TPU v7x, 256 devices: a whole 4x4x8 slice. The times are simulated.
256 devices in a mesh: wide: 32 (over y_lo, z, core), narrow: 8 (over y_hi, x).
Axes of the slice: x: 4, y: 4 (y_hi: 2, y_lo: 2; y = y_hi * 2 + y_lo), z: 8, core: 2. Of those that a mesh axis runs over, the one named last changes fastest.
Arguments:
- compound_activation: bfloat16 [8, 5120, 2048], P('narrow', 'wide'), may hold values from -0.29882812 to 0.29882812
- compound_vectors: bfloat16 [8, 5120, 1024], P('narrow', 'wide'), may hold values from -2.34375 to 2.34375
- pathway_vectors: bfloat16 [8, 5120, 1024], P('narrow', 'wide'), may hold values from -2.34375 to 2.34375
- matching_pathway_index: int32 [8, 5120], P('narrow', 'wide'), may hold values from 0 to 5119, each once within a row
- exponent_of_sharpness: float32 [1], replicated, may hold values from 3.4 to 4.1
- offset_shift: float32 [1], replicated, may hold values from -4 to -2
- objective_seed: float32 [1], replicated, may hold values from 0.05 to 0.2
Outputs:
- weight_grad: float32 [2048, 1024], P('wide')
- route_grad: bfloat16 [8, 5120, 1024], P('narrow', 'wide')
All inputs are finite; a program needn't handle non-finite values.
Results may differ from a plain program's by a relative error of at most 0.006.
Values may be sent and summed in bfloat16 or wider, within the bound.
A program may use at most 64 MiB of HBM per device.

v0:
```python
import jax
import jax.numpy as jnp
from jax import lax
from jax.sharding import PartitionSpec as P


def unit_rows(embed):
    values = embed.astype(jnp.float32)
    magnitude = jnp.sqrt(jnp.sum(values * values, -1, keepdims=True) + 1e-06)
    return (values / magnitude, magnitude)


def unit_back(unit_f, magnitude, upstream_grad):
    along = jnp.sum(unit_f * upstream_grad, -1, keepdims=True)
    return (upstream_grad - unit_f * along) / magnitude


def contract_rows(left_rows, right_rows):
    return lax.dot_general(
        left_rows, right_rows, (((0,), (0,)), ((), ())), preferred_element_type=jnp.float32
    )


def local(
    compound_activation,
    compound_vectors,
    pathway_vectors,
    matching_pathway_index,
    exponent_of_sharpness,
    offset_shift,
    objective_seed,
):
    score_sharpness = jnp.exp(exponent_of_sharpness[0])
    score_shift_amount = offset_shift[0]
    incoming_adjoint = objective_seed[0]
    hidden = compound_activation[0]
    targets_own = matching_pathway_index[0]
    mol_unit_f, mol_length = unit_rows(compound_vectors[0])
    route_unit_f, route_length = unit_rows(pathway_vectors[0])
    compound_normed_vectors = mol_unit_f.astype(jnp.bfloat16)
    pathway_normed_vectors = route_unit_f.astype(jnp.bfloat16)
    incoming = lax.all_gather(pathway_normed_vectors, "wide", axis=0, tiled=True)
    similarity_grid = lax.dot_general(
        compound_normed_vectors,
        incoming,
        (((1,), (1,)), ((), ())),
        preferred_element_type=jnp.float32,
    )
    col_ids = jnp.arange(incoming.shape[0], dtype=jnp.int32)
    matching_mask = (col_ids[None, :] == targets_own[:, None]).astype(jnp.float32)
    gradient_patch = (
        incoming_adjoint
        * (jax.nn.sigmoid(score_sharpness * similarity_grid + score_shift_amount) - matching_mask)
    ).astype(jnp.bfloat16)
    aggregate_objective = jnp.dot(gradient_patch, incoming, preferred_element_type=jnp.float32)
    compound_normed_derivative = score_sharpness * aggregate_objective
    grad_cols = lax.all_to_all(gradient_patch, "wide", split_axis=1, concat_axis=0, tiled=True)
    pathway_derivative_sum = contract_rows(
        grad_cols, lax.all_gather(compound_normed_vectors, "wide", axis=0, tiled=True)
    )
    pathway_normed_derivative = score_sharpness * pathway_derivative_sum
    mol_dembed = unit_back(mol_unit_f, mol_length, compound_normed_derivative).astype(jnp.bfloat16)
    route_dembed = unit_back(route_unit_f, route_length, pathway_normed_derivative).astype(
        jnp.bfloat16
    )
    partial_value = lax.psum_scatter(
        contract_rows(hidden, mol_dembed), "wide", scatter_dimension=0, tiled=True
    )
    weight_grad = lax.psum(partial_value, "narrow")
    return (weight_grad, route_dembed[None])


def solution(mesh):
    in_specs = (
        P("narrow", "wide", None),
        P("narrow", "wide", None),
        P("narrow", "wide", None),
        P("narrow", "wide"),
        P(),
        P(),
        P(),
    )
    out_specs = (P("wide", None), P("narrow", "wide", None))
    return jax.shard_map(local, mesh=mesh, in_specs=in_specs, out_specs=out_specs, check_vma=False)
```

profile of v0, /device:TPU:2, one launch (start us, length us, event | category | flops | bytes accessed | tf_op | source)
XLA Modules:
  0.0 448.7 jit_solution(5760545285905820272)
XLA Ops:
  7.2 0.0 copy-start
  7.2 0.0 all-gather.3.cloned.1.call-start
  7.2 1.2 fusion.9
  8.4 1.8 fusion.15
  10.2 0.0 all-gather.3.cloned.1.call-update
  10.3 0.0 reduce-scatter.4.cloned.1.call-start
  12.3 1.1 fusion.8
  13.4 1.1 fusion.14
  14.5 0.0 copy-start.4
  14.6 73.7 %all-gather.3.cloned.1.call-done = bf16[5120,1024]{1,0:T(8,128)(2,1)} async-done(((bf16[160,1024]{1,0:T(8,128)(2,1)}), bf16[5120,1024]{1,0:T(8,128)(2,1)}) %all-gather.3.cloned.1.call-update) | async-done | bytes 10485776 | tf_op jit(solution)/shard_map/all_gather | solution.py:42
  88.2 8.4 %fusion.7 = bf16[160,5120]{1,0:T(8,128)(2,1)S(1)} fusion(bf16[160,1024]{1,0:T(8,128)(2,1)S(1)} %fusion.14, bf16[5120,1024]{1,0:T(8,128)(2,1)} %all-gather.3.cloned.1.call-done, s32[160]{0:T(256)} %bitcast.47, f32[]{:T(128)} %bitcast.43, f32[]{:T(128)} %bitcast, f32[]{:T(128)} %bitcast.44), kind=kOutput, calls=%fused_computation.8 | convolution fusion | flops 1685913600 | bytes 12452492 | tf_op jit(solution)/shard_map/dot_general | solution.py:43
  96.7 0.0 copy-done.4
  96.7 2.1 multiply_reduce_fusion.1
  98.8 4.6 %convolution_bitcast_fusion = f32[2048,1024]{0,1:T(8,128)} fusion(bf16[1,160,2048]{2,1,0:T(8,128)(2,1)S(1)} %copy-done, f32[160,1024]{1,0:T(8,128)S(1)} %get-tuple-element.9, f32[160]{0:T(256)S(1)} %get-tuple-element.8, f32[160]{0:T(256)S(1)} %add_sqrt_fusion.1, bf16[1,160,1024]{2,1,0:T(8,128)(2,1)S(1)} %copy-done.1), kind=kOutput, calls=%fused_computation.9 | convolution fusion | flops 672071680 | bytes 10028288 | tf_op jit(solution)/shard_map/dot_general | solution.py:19
  103.4 9.3 %copy.16 = f32[2048,1024]{1,0:T(8,128)} copy(f32[2048,1024]{0,1:T(8,128)} %convolution_bitcast_fusion) | data formatting | bytes 16777216
  112.7 0.0 reduce-scatter.4.cloned.1.call-update
  112.7 0.0 all-gather.5.cloned.1.call-start
  112.7 0.7 all-gather.5.cloned.1.call-update
  113.4 0.0 all-reduce.2.cloned.1.call-start
  113.5 3.0 copy.15
  116.5 82.3 %all_to_all.19 = bf16[160,32,160]{0,2,1:T(8,128)(2,1)S(1)} all-to-all(bf16[160,32,160]{0,2,1:T(8,128)(2,1)S(1)} %bitcast.45), channel_id=1, replica_groups=mesh['wide'=32,'narrow'=8] {'wide'}, dimensions={1} | all-to-all | bytes 3276800 | tf_op jit(solution)/shard_map/all_to_all | solution.py:57
  198.8 1.5 copy.13
  200.3 4.7 %all_to_all.17 = bf16[5120,160]{0,1:T(8,128)(2,1)} reshape(bf16[32,160,160]{1,0,2:T(8,128)(2,1)S(1)} %copy.13) | data formatting | bytes 3276800 | tf_op jit(solution)/shard_map/all_to_all | solution.py:57
  205.1 73.4 %reduce-scatter.4.cloned.1.call-done = f32[64,1024]{1,0:T(8,128)} async-done(((f32[2048,1024]{1,0:T(8,128)}), f32[64,1024]{1,0:T(8,128)}) %reduce-scatter.4.cloned.1.call-update) | async-done | bytes 262160
  278.4 2.0 copy.17
  280.4 0.0 all-reduce.2.cloned.1.call-update
  280.4 0.0 copy-start.2
  280.4 70.9 %all-gather.5.cloned.1.call-done = bf16[5120,1024]{1,0:T(8,128)(2,1)} async-done(((bf16[160,1024]{1,0:T(8,128)(2,1)}), bf16[5120,1024]{1,0:T(8,128)(2,1)}) %all-gather.5.cloned.1.call-update) | async-done | bytes 10485776 | tf_op jit(solution)/shard_map/all_gather | solution.py:59
  351.3 6.5 %multiply_reduce_fusion = (f32[160]{0:T(256)S(1)}, f32[160,1024]{1,0:T(8,128)S(1)}) fusion(f32[160]{0:T(256)S(1)} %add_sqrt_fusion, bf16[1,160,1024]{2,1,0:T(8,128)(2,1)} %param.9, bf16[5120,160]{0,1:T(8,128)(2,1)} %all_to_all.17, bf16[5120,1024]{1,0:T(8,128)(2,1)} %all-gather.5.cloned.1.call-done, f32[]{:T(128)} %bitcast), kind=kOutput, calls=%fused_computation.21 | convolution fusion | flops 1678540672 | bytes 13108484 | tf_op jit(solution)/shard_map/dot_general | solution.py:19
  357.8 0.9 fusion.13
  358.8 81.5 %all-reduce.2.cloned.1.call-done = f32[64,1024]{0,1:T(8,128)} async-done(((f32[64,1024]{0,1:T(8,128)}), f32[64,1024]{0,1:T(8,128)}) %all-reduce.2.cloned.1.call-update) | async-done | bytes 262160 | tf_op jit(solution)/shard_map/psum | solution.py:69
  440.3 1.9 copy.14
  (10 shorter events, 0.0 us)
Async XLA Ops:
  7.2 91.6 %copy-start = (bf16[1,160,2048]{2,1,0:T(8,128)(2,1)S(1)}, bf16[1,160,2048]{2,1,0:T(8,128)(2,1)}, u32[]{:S(2)}) copy-start(bf16[1,160,2048]{2,1,0:T(8,128)(2,1)} %param.7) | copy-start | bytes 1966084
  7.2 81.1 %all-gather.3.cloned.1.call-start = ((), (), s32[]{:S(2)}) async-start(), calls=%async_computation.2 | async-start | bytes 10813440 | tf_op jit(solution)/shard_map/all_gather | solution.py:42
  10.3 268.1 %reduce-scatter.4.cloned.1.call-start = ((), (), s32[]{:S(2)}) async-start(), calls=%async_computation.5 | async-start | bytes 8650752
  14.5 82.1 %copy-start.4 = (bf16[160,1024]{1,0:T(8,128)(2,1)}, bf16[160,1024]{1,0:T(8,128)(2,1)S(1)}, u32[]{:S(2)}) copy-start(bf16[160,1024]{1,0:T(8,128)(2,1)S(1)} %fusion.14) | copy-start | bytes 983044
  88.2 8.4 %copy-start.1 = (bf16[1,160,1024]{2,1,0:T(8,128)(2,1)S(1)}, bf16[1,160,1024]{2,1,0:T(8,128)(2,1)}, u32[]{:S(2)}) copy-start(bf16[1,160,1024]{2,1,0:T(8,128)(2,1)} %param.8) | copy-start | bytes 983044
  88.2 8.4 %copy-start.5 = (bf16[5120,1024]{1,0:T(8,128)(2,1)S(1)}, bf16[5120,1024]{1,0:T(8,128)(2,1)}, u32[]{:S(2)}) copy-start(bf16[5120,1024]{1,0:T(8,128)(2,1)} %all-gather.3.cloned.1.call-done) | copy-start | bytes 31457284
  96.7 2.1 copy-start.3
  112.7 238.7 %all-gather.5.cloned.1.call-start = ((), (), s32[]{:S(2)}) async-start(), calls=%async_computation.4 | async-start | bytes 10813440 | tf_op jit(solution)/shard_map/all_gather | solution.py:59
  113.4 326.9 %all-reduce.2.cloned.1.call-start = ((), (), s32[]{:S(2)}) async-start(), calls=%async_computation.3 | async-start | bytes 1048576 | tf_op jit(solution)/shard_map/psum | solution.py:69
  280.4 77.4 %copy-start.2 = (bf16[1,160,1024]{2,1,0:T(8,128)(2,1)S(1)}, bf16[1,160,1024]{2,1,0:T(8,128)(2,1)}, u32[]{:S(2)}) copy-start(bf16[1,160,1024]{2,1,0:T(8,128)(2,1)} %param.9) | copy-start | bytes 983044
Sparse Core Ops, SparseCore 0:
  10.4 77.7 all-gather.2
  112.8 165.5 reduce-scatter.3
  280.3 71.0 all-gather.4
  353.8 86.4 all-reduce.1
where the time goes:
time: 452 us; the launch traced here: 449 us
  waiting for transfers between devices  300 us (66%)
  blocking collectives  82.3 us (18%)
  local copies, waits for them, and re-layouts  22.4 us (5%)
  matrix products  21.6 us (5%)
  between operations  15.9 us (4%)
  other arithmetic  6.21 us (1%)
    all_to_all x1, blocking collectives, local(): lax.all_to_all(gradient_patch, 'wide', split_axis=1, concat_axis=0, tiled...  82.3 us
    psum x1, waiting for transfers between devices, local(): weight_grad = lax.psum(partial_value, 'narrow')  81.5 us
    unnamed x5, waiting for transfers between devices  74.1 us
    all_gather x1, waiting for transfers between devices, local(): lax.all_gather(pathway_normed_vectors, 'wide', axis=0, tiled=True)  73.7 us
    all_gather x1, waiting for transfers between devices, local(): lax.all_gather(compound_normed_vectors, 'wide', axis=0, tiled=True)  70.9 us
    unnamed x15, local copies, waits for them, and re-layouts  13.2 us
    dot_general x2, matrix products, contract_rows(): lax.dot_general(left_rows, right_rows, (((0,), (0,)), ((), ())), preferre...  11.1 us
    all_to_all x3, local copies, waits for them, and re-layouts, local(): lax.all_to_all(gradient_patch, 'wide', split_axis=1, concat_axis=0, tiled...  9.24 us
  transfers between devices with their start and end apart: 4, of which 4 were waited for; matrix products, arithmetic and copies ran while one was open for 4% of the time, Pallas kernels for 0%

commit v1 on v0

v1 whole, which is shorter than its diff:
```python
import jax
import jax.numpy as jnp
from jax import lax
from jax.experimental import pallas as pl
from jax.experimental.pallas import tpu as pltpu
from jax.sharding import PartitionSpec as P

ROWS = 160
HALF = 80
D = 1024
FF = 2048
PAIR = 2 * ROWS
F32 = jnp.float32
BF16 = jnp.bfloat16
MESH = pl.DeviceIdType.MESH
NT = (((1,), (1,)), ((), ()))
NN = (((1,), (0,)), ((), ()))


def wide_of(y, z, c):
    return y * 16 + z * 2 + c


def wrap(i, n):
    return lax.rem(i + n, n)


def loop(n, body):
    lax.fori_loop(0, n, lambda i, _: (body(i), 0)[1], 0)


def kernel(
    act_ref,
    mol_ref,
    route_ref,
    target_ref,
    sharp_ref,
    shift_ref,
    seed_ref,
    weight_out,
    route_out,
    ring_r,
    ring_m,
    cross_m,
    cross_r,
    tring,
    tcross,
    tcol,
    part_m,
    part_r,
    sib_in,
    y_out,
    y_in,
    a_out,
    a_in,
    act_t,
    act_own,
    act_sib,
    mold,
    wsend,
    wrecv,
    zsend,
    zrecv,
    gath,
    ring_ss,
    ring_rs,
    cross_ss,
    cross_rs,
    t_ss,
    t_rs,
    red_ss,
    red_rs,
    mis_ss,
    mis_rs,
    w_ss,
    w_rs,
    z_ss,
    z_rs,
    g_ss,
    g_rs,
):
    w = lax.axis_index("wide")
    n = lax.axis_index("narrow")
    y = lax.div(w, 16)
    z = lax.rem(lax.div(w, 2), 8)
    c = lax.rem(w, 2)
    q = 2 * y + c
    e = y * 8 + n
    sib = (wide_of(y, z, 1 - c), n)
    across = (wide_of(1 - y, z, c), n)
    diag = (wide_of(1 - y, z, 1 - c), n)
    zpeer = [(wide_of(y, wrap(z + k, 8), c), n) for k in range(1, 8)]

    def w_index(r):
        return lax.rem(e + r + 16, 16)

    def w_peer(r):
        d = w_index(r)
        return (wide_of(lax.div(d, 8), z, c), lax.rem(d, 8))

    def n_peer(k):
        return (w, lax.rem(n + k, 8))

    barrier = pltpu.get_barrier_semaphore()
    partners = zpeer + [sib, diag] + [w_peer(r) for r in range(1, 16)]
    for dev in partners:
        pl.semaphore_signal(barrier, inc=1, device_id=dev, device_id_type=MESH)

    sent = []

    def remote(src, dst, ss, rs, dev):
        return pltpu.make_async_remote_copy(
            src_ref=src, dst_ref=dst, send_sem=ss, recv_sem=rs, device_id=dev, device_id_type=MESH
        )

    def send(*a):
        cp = remote(*a)
        cp.start()
        sent.append(cp)

    def block(q_):
        return pl.ds(pl.multiple_of(q_ * ROWS, ROWS), ROWS)

    def normalise(raw, ring, cross):
        def body(i):
            rows = pl.ds(pl.multiple_of(i * 32, 32), 32)
            v = raw[rows, :].astype(F32)
            inv = 1.0 / jnp.sqrt(jnp.sum(v * v, -1, keepdims=True) + 1e-06)
            u = (v * inv).astype(BF16)
            ring[z, rows, :] = u
            cross[pl.ds(pl.multiple_of(q * ROWS + i * 32, 32), 32), :] = u

        loop(ROWS // 32, body)

    normalise(route_ref, ring_r, cross_r)
    normalise(mol_ref, ring_m, cross_m)
    t_own = jnp.concatenate(
        [target_ref[...].astype(F32), jnp.zeros((1, 256 - ROWS), F32)], axis=1
    )
    t_own = jnp.broadcast_to(t_own, (8, 256))
    tring[z] = t_own
    tcross[q] = t_own

    pl.semaphore_wait(barrier, len(partners))

    rings = (ring_r, ring_m)

    def exists(d, k, h):
        return k < 3 or (k == 3 and h == d)

    def ring_copy(a, d, k, h, slot):
        i = ((a * 2 + d) * 4 + k) * 2 + h
        part = rings[a].at[slot, pl.ds(h * HALF, HALF)]
        dev = zpeer[0] if d == 0 else zpeer[6]
        return remote(part, part, ring_ss.at[i], ring_rs.at[i], dev)

    def ring_send(a, d, k, h):
        cp = ring_copy(a, d, k, h, wrap(z - k, 8) if d == 0 else wrap(z + k, 8))
        cp.start()
        sent.append(cp)

    def ring_wait(a, d, k, h):
        ring_copy(a, d, k, h, wrap(z - 1 - k, 8) if d == 0 else wrap(z + 1 + k, 8)).wait_recv()

    def advance(a, k, pieces=(0, 1)):
        for h in pieces:
            for d in (0, 1):
                if exists(d, k, h):
                    ring_wait(a, d, k, h)
                    if exists(d, k + 1, h):
                        ring_send(a, d, k + 1, h)

    def ring_open(a):
        for h in (0, 1):
            for d in (0, 1):
                ring_send(a, d, 0, h)

    crosses = (cross_m, cross_r)
    b_own, b_sib = block(q), block(2 * y + 1 - c)
    b_across, b_diag = block(2 * (1 - y) + c), block(2 * (1 - y) + 1 - c)

    def cross_copy(a, i, blk, dev):
        part = crosses[a].at[blk]
        return remote(part, part, cross_ss.at[a * 3 + i], cross_rs.at[a * 3 + i], dev)

    def cross_send(a, i):
        cp = cross_copy(a, i, b_across if i == 2 else b_own, across if i == 0 else sib)
        cp.start()
        sent.append(cp)

    def cross_wait(a, i):
        cross_copy(a, i, (b_across, b_sib, b_diag)[i], sib).wait_recv()

    for k in range(1, 8):
        send(tring.at[z], tring.at[z], t_ss.at[k - 1], t_rs.at[k - 1], zpeer[k - 1])
    for i, dev in enumerate((sib, across, diag)):
        send(tcross.at[q], tcross.at[q], t_ss.at[7 + i], t_rs.at[7 + i], dev)

    cross_send(0, 0)
    ring_open(0)
    cross_send(0, 1)

    for t in range(16):
        tile = act_ref[:, 128 * t : 128 * t + 128].astype(F32)
        act_t[128 * t : 128 * t + 128, :] = tile.T

    def order(j):
        yy, nn = lax.div(j, 8), lax.rem(j, 8)
        for h in (0, 1):
            parts = [
                act_t[pl.ds(pl.multiple_of(1024 * yy + 128 * zz + 64 * h + 8 * nn, 8), 8), :]
                for zz in range(8)
            ]
            act_own[h, pl.ds(pl.multiple_of(j * 64, 64), 64), :] = jnp.concatenate(
                parts, axis=0
            ).astype(BF16)

    loop(16, order)
    send(act_own.at[1 - c], act_sib, mis_ss.at[0], mis_rs.at[0], sib)

    advance(0, 0)
    cross_wait(0, 0)
    cross_send(0, 2)

    for k in range(1, 8):
        slot = wrap(z - k, 8)
        remote(
            tring.at[slot], tring.at[slot], t_ss.at[k - 1], t_rs.at[k - 1], sib
        ).wait_recv()
    for i, slot in enumerate((2 * y + 1 - c, 2 * (1 - y) + c, 2 * (1 - y) + 1 - c)):
        remote(
            tcross.at[slot], tcross.at[slot], t_ss.at[7 + i], t_rs.at[7 + i], sib
        ).wait_recv()
    eye = lax.broadcasted_iota(jnp.int32, (ROWS, ROWS), 0) == lax.broadcasted_iota(
        jnp.int32, (ROWS, ROWS), 1
    )
    for i in range(4):
        line = jnp.broadcast_to(tcross[i, 0:1, 0:ROWS], (ROWS, ROWS))
        col = jnp.sum(jnp.where(eye, line, 0.0), -1, keepdims=True)
        tcol[i * ROWS : (i + 1) * ROWS, :] = jnp.broadcast_to(col, (ROWS, 128))

    cross_wait(0, 1)
    cross_wait(0, 2)

    shift = shift_ref[0]
    seed = seed_ref[0]
    parts = (part_m, part_r)

    def pairs(a, slot, first):
        def body(b):
            rows = pl.ds(pl.multiple_of(b * PAIR, PAIR), PAIR)
            right = rings[a][slot]
            sharp = jnp.exp(jnp.full((1, ROWS), sharp_ref[0], F32))
            s = lax.dot_general(crosses[a][rows, :], right, NT, preferred_element_type=F32)
            if a == 0:
                base = wide_of(y, slot, c) * ROWS
                ids = lax.broadcasted_iota(jnp.int32, (1, ROWS), 1) + base
                match = tcol[rows, 0:1] == ids.astype(F32)
            else:
                base = wide_of(b, z, 0) * ROWS
                ids = lax.broadcasted_iota(jnp.int32, (PAIR, 1), 0) + base
                match = ids.astype(F32) == tring[slot, 0:1, 0:ROWS]
            g = jax.nn.sigmoid(s * sharp + shift) - jnp.where(match, 1.0, 0.0)
            g = (seed * g).astype(BF16)
            out = lax.dot_general(g, right, NN, preferred_element_type=F32)
            if first:
                parts[a][rows, :] = out
            else:
                parts[a][rows, :] += out

        loop(2, body)

    def pairs_at(a, k):
        loop(2, lambda i: pairs(a, wrap(z + (2 * i - 1) * k, 8), False))

    def reduce_open(a):
        send(parts[a].at[b_diag], sib_in.at[a, 0], red_ss.at[a * 4], red_rs.at[a * 4], sib)
        send(parts[a].at[b_sib], sib_in.at[a, 1], red_ss.at[a * 4 + 1], red_rs.at[a * 4 + 1], sib)

    def reduce_wait(a, i):
        dst = (sib_in.at[a, 0], sib_in.at[a, 1], y_in.at[a], a_in.at[a])[i]
        remote(dst, dst, red_ss.at[a * 4 + i], red_rs.at[a * 4 + i], sib).wait_recv()

    def reduce_across(a):
        reduce_wait(a, 0)

        def body(i):
            rows = pl.ds(pl.multiple_of(i * 32, 32), 32)
            far = pl.ds(pl.multiple_of((2 * (1 - y) + c) * ROWS + i * 32, 32), 32)
            total = parts[a][far, :] + sib_in[a, 0, rows, :]
            unit = crosses[a][far, :].astype(F32)
            along = jnp.sum(total * unit, -1, keepdims=True)
            y_out[a, rows, :] = (total - along * unit).astype(BF16)
            a_out[a, rows, :] = jnp.broadcast_to(along, (32, 128))

        loop(ROWS // 32, body)
        send(y_out.at[a], y_in.at[a], red_ss.at[a * 4 + 2], red_rs.at[a * 4 + 2], across)
        send(a_out.at[a], a_in.at[a], red_ss.at[a * 4 + 3], red_rs.at[a * 4 + 3], across)

    def reduce_close(a, raw, put):
        reduce_wait(a, 1)
        reduce_wait(a, 2)
        reduce_wait(a, 3)

        def body(i):
            rows = pl.ds(pl.multiple_of(i * 32, 32), 32)
            own = pl.ds(pl.multiple_of(q * ROWS + i * 32, 32), 32)
            sharp = jnp.exp(jnp.full((32, 1), sharp_ref[0], F32))
            total = parts[a][own, :] + sib_in[a, 1, rows, :] + y_in[a, rows, :].astype(F32)
            total = total + a_in[a, rows, 0:1] * crosses[a][own, :].astype(F32)
            v = raw[rows, :].astype(F32)
            inv = 1.0 / jnp.sqrt(jnp.sum(v * v, -1, keepdims=True) + 1e-06)
            unit = v * inv
            along = jnp.sum(unit * total, -1, keepdims=True)
            put(i, ((total - unit * along) * (inv * sharp)).astype(BF16))

        loop(ROWS // 32, body)

    pairs(0, z, True)
    pairs_at(0, 1)
    advance(0, 1)
    cross_send(1, 0)
    cross_send(1, 1)
    pairs_at(0, 2)
    advance(0, 2)
    ring_open(1)
    pairs_at(0, 3)
    cross_wait(1, 0)
    cross_send(1, 2)
    advance(0, 3)
    pairs(0, wrap(z + 4, 8), False)

    reduce_open(0)
    advance(1, 0, (0,))
    reduce_across(0)
    cross_wait(1, 1)
    cross_wait(1, 2)
    pairs(1, z, True)
    advance(1, 0, (1,))
    pairs_at(1, 1)
    advance(1, 1, (0,))

    def put_mold(i, value):
        mold[c, pl.ds(pl.multiple_of(i * 32, 32), 32), :] = value

    reduce_close(0, mol_ref, put_mold)
    send(mold.at[c], mold.at[c], mis_ss.at[1], mis_rs.at[1], sib)
    advance(1, 1, (1,))
    remote(act_sib, act_sib, mis_ss.at[0], mis_rs.at[0], sib).wait_recv()
    remote(mold.at[1 - c], mold.at[1 - c], mis_ss.at[1], mis_rs.at[1], sib).wait_recv()

    def weight(i):
        cols = pl.ds(pl.multiple_of(i * 256, 256), 256)
        prod = lax.dot_general(act_own[c], mold[c, :, cols], NN, preferred_element_type=F32)
        prod += lax.dot_general(act_sib[...], mold[1 - c, :, cols], NN, preferred_element_type=F32)
        wsend[:, :, cols] = prod.astype(BF16).reshape(16, 64, 256)

    loop(4, weight)
    for r in range(1, 16):
        send(wsend.at[w_index(r)], wrecv.at[e], w_ss.at[r - 1], w_rs.at[r - 1], w_peer(r))

    advance(1, 2, (0,))
    pairs_at(1, 2)
    advance(1, 2, (1,))
    pairs_at(1, 3)
    advance(1, 3)
    pairs(1, wrap(z + 4, 8), False)
    reduce_open(1)
    reduce_across(1)

    for r in range(1, 16):
        slot = w_index(-r)
        remote(
            wrecv.at[slot], wrecv.at[slot], w_ss.at[r - 1], w_rs.at[r - 1], sib
        ).wait_recv()

    def gather_sum(i):
        rows = pl.ds(pl.multiple_of(i * 16, 16), 16)
        total = wsend[e, rows, :].astype(F32)
        for r in range(1, 16):
            total += wrecv[w_index(-r), rows, :].astype(F32)
        zsend[rows, :] = total

    loop(4, gather_sum)
    for k in range(1, 8):
        src = zsend.at[pl.ds(pl.multiple_of(wrap(z + k, 8) * 8, 8), 8)]
        send(src, zrecv.at[z], z_ss.at[k - 1], z_rs.at[k - 1], zpeer[k - 1])

    def put_route(i, value):
        route_out[pl.ds(pl.multiple_of(i * 32, 32), 32), :] = value

    reduce_close(1, route_ref, put_route)

    total = zsend[pl.ds(pl.multiple_of(z * 8, 8), 8), :]
    for k in range(1, 8):
        slot = wrap(z - k, 8)
        remote(
            zrecv.at[slot], zrecv.at[slot], z_ss.at[k - 1], z_rs.at[k - 1], sib
        ).wait_recv()
        total += zrecv[slot]
    gath[n] = total
    for k in range(1, 8):
        send(gath.at[n], gath.at[n], g_ss.at[k - 1], g_rs.at[k - 1], n_peer(k))
    for k in range(1, 8):
        slot = wrap(n - k, 8)
        remote(
            gath.at[slot], gath.at[slot], g_ss.at[k - 1], g_rs.at[k - 1], sib
        ).wait_recv()
    weight_out[...] = gath[...].reshape(64, D)
    for cp in sent:
        cp.wait_send()


def local(
    compound_activation,
    compound_vectors,
    pathway_vectors,
    matching_pathway_index,
    exponent_of_sharpness,
    offset_shift,
    objective_seed,
):
    vmem = pl.BlockSpec(memory_space=pltpu.VMEM)
    smem = pl.BlockSpec(memory_space=pltpu.SMEM)
    dma = pltpu.SemaphoreType.DMA
    weight_grad, route_grad = pl.pallas_call(
        kernel,
        out_shape=(
            jax.ShapeDtypeStruct((64, D), F32),
            jax.ShapeDtypeStruct((ROWS, D), BF16),
        ),
        in_specs=[vmem] * 4 + [smem] * 3,
        out_specs=(vmem, vmem),
        scratch_shapes=[
            pltpu.VMEM((8, ROWS, D), BF16),
            pltpu.VMEM((8, ROWS, D), BF16),
            pltpu.VMEM((4 * ROWS, D), BF16),
            pltpu.VMEM((4 * ROWS, D), BF16),
            pltpu.VMEM((8, 8, 256), F32),
            pltpu.VMEM((4, 8, 256), F32),
            pltpu.VMEM((4 * ROWS, 128), F32),
            pltpu.VMEM((4 * ROWS, D), F32),
            pltpu.VMEM((4 * ROWS, D), F32),
            pltpu.VMEM((2, 2, ROWS, D), F32),
            pltpu.VMEM((2, ROWS, D), BF16),
            pltpu.VMEM((2, ROWS, D), BF16),
            pltpu.VMEM((2, ROWS, 128), F32),
            pltpu.VMEM((2, ROWS, 128), F32),
            pltpu.VMEM((FF, ROWS), F32),
            pltpu.VMEM((2, FF // 2, ROWS), BF16),
            pltpu.VMEM((FF // 2, ROWS), BF16),
            pltpu.VMEM((2, ROWS, D), BF16),
            pltpu.VMEM((16, 64, D), BF16),
            pltpu.VMEM((16, 64, D), BF16),
            pltpu.VMEM((64, D), F32),
            pltpu.VMEM((8, 8, D), F32),
            pltpu.VMEM((8, 8, D), F32),
            dma((32,)),
            dma((32,)),
            dma((6,)),
            dma((6,)),
            dma((10,)),
            dma((10,)),
            dma((8,)),
            dma((8,)),
            dma((2,)),
            dma((2,)),
            dma((15,)),
            dma((15,)),
            dma((7,)),
            dma((7,)),
            dma((7,)),
            dma((7,)),
        ],
        compiler_params=pltpu.CompilerParams(
            collective_id=0, has_side_effects=True, vmem_limit_bytes=48 * 1024 * 1024
        ),
        name="contrastive_backward",
    )(
        compound_activation[0],
        compound_vectors[0],
        pathway_vectors[0],
        matching_pathway_index,
        exponent_of_sharpness,
        offset_shift,
        objective_seed,
    )
    return weight_grad, route_grad[None]


def solution(mesh):
    in_specs = (
        P("narrow", "wide", None),
        P("narrow", "wide", None),
        P("narrow", "wide", None),
        P("narrow", "wide"),
        P(),
        P(),
        P(),
    )
    out_specs = (P("wide", None), P("narrow", "wide", None))
    return jax.shard_map(local, mesh=mesh, in_specs=in_specs, out_specs=out_specs, check_vma=False)
```

time: 452 us -> 119 us (0.26)
  waiting for transfers between devices: 300 us -> 0 us
  Pallas kernels: 0 us -> 110 us
  blocking collectives: 82.3 us -> 0 us
  matrix products: 21.6 us -> 0 us
  local copies, waits for them, and re-layouts: 22.4 us -> 5.13 us
  between operations: 15.9 us -> 2.59 us
  other arithmetic: 6.21 us -> 0 us
    all_gather x2 -> x0, waiting for transfers between devices: 145 us -> none  [the longest x1 73.7 us: local(): lax.all_gather(pathway_normed_vectors, 'wide', axis=0, tiled=True)]
    pallas_call x0 -> x1, Pallas kernels: none -> 110 us  [local(): pl.pallas_call(kernel, out_shape=(jax.ShapeDtypeStruct((64, D), F32), jax...]
    all_to_all x1 -> x0, blocking collectives: 82.3 us -> none  [local(): lax.all_to_all(gradient_patch, 'wide', split_axis=1, concat_axis=0, tiled...]
    psum x1 -> x0, waiting for transfers between devices: 81.5 us -> none  [local(): weight_grad = lax.psum(partial_value, 'narrow')]
    unnamed x5 -> x0, waiting for transfers between devices: 74.1 us -> none
    dot_general x4 -> x0, matrix products: 21.5 us -> none  [the longest x2 11.1 us: contract_rows(): lax.dot_general(left_rows, right_rows, (((0,), (0,)), ((), ())), preferre...]
    all_to_all x3 -> x0, local copies, waits for them, and re-layouts: 9.24 us -> none  [local(): lax.all_to_all(gradient_patch, 'wide', split_axis=1, concat_axis=0, tiled...]
    unnamed x15 -> x10, local copies, waits for them, and re-layouts: 13.2 us -> 5.13 us
  transfers between devices with their start and end apart: 4 -> 0, of which waited for: 4 -> 0; matrix products, arithmetic and copies ran while one was open for 4% -> 0% of each run, Pallas kernels for 0% -> 0%
where the time goes in v1:
time: 119 us; the launch traced here: 117 us
  Pallas kernels  110 us (92%)
  local copies, waits for them, and re-layouts  5.13 us (4%)
  between operations  2.59 us (2%)
    pallas_call x1, Pallas kernels, local(): pl.pallas_call(kernel, out_shape=(jax.ShapeDtypeStruct((64, D), F32), jax...  110 us
    unnamed x10, local copies, waits for them, and re-layouts  5.13 us

profile of v1, /device:TPU:2, one launch (start us, length us, event | category | flops | bytes accessed | tf_op | source)
XLA Modules:
  0.0 117.4 jit_solution(797588780743104301)
XLA Ops:
  2.6 0.0 copy-start.3
  2.6 0.7 copy-done.3
  3.2 0.0 copy-start
  3.2 1.1 copy-done
  4.3 0.0 copy-start.1
  4.3 1.0 copy-done.1
  5.3 0.0 copy-start.2
  5.3 1.0 copy-done.2
  6.3 109.6 %contrastive_backward.1 = (f32[64,1024]{1,0:T(8,128)S(1)}, bf16[160,1024]{1,0:T(8,128)(2,1)S(1)}) custom-call(bf16[160,2048]{1,0:T(8,128)(2,1)S(1)} %bitcast.4, bf16[160,1024]{1,0:T(8,128)(2,1)S(1)} %bitcast.6, bf16[160,1024]{1,0:T(8,128)(2,1)S(1)} %bitcast.7, s32[1,160]{1,0:T(1,128)S(1)} %copy-done.3, f32[1]{0:T(128)S(6)} %copy.11.sharp_ref, ...), custom_call_target="tpu_custom_call" | custom-call | tf_op jit(solution)/shard_map/contrastive_backward/pallas_call | solution.py:426
  115.9 0.7 copy.14
  116.6 0.7 copy.15
Async XLA Ops:
  2.6 0.7 copy-start.3
  3.2 1.1 copy-start
  4.3 1.0 copy-start.1
  5.3 1.0 copy-start.2

commit v2 on v1

--- a/solution.py
+++ b/solution.py
@@ -30,15 +30,18 @@
 
 
 def kernel(
-    act_ref,
-    mol_ref,
-    route_ref,
+    act_hbm,
+    mol_hbm,
+    route_hbm,
     target_ref,
     sharp_ref,
     shift_ref,
     seed_ref,
     weight_out,
     route_out,
+    act_ref,
+    mol_ref,
+    route_ref,
     ring_r,
     ring_m,
     cross_m,
@@ -55,10 +58,14 @@
     a_in,
     act_t,
     act_own,
-    act_sib,
-    mold,
+    act_x,
+    act_y,
+    mold_x,
+    mold_y,
+    prod,
     wsend,
     wrecv,
+    zown,
     zsend,
     zrecv,
     gath,
@@ -70,8 +77,11 @@
     t_rs,
     red_ss,
     red_rs,
-    mis_ss,
-    mis_rs,
+    in_s,
+    act_ss,
+    act_rs,
+    mold_ss,
+    mold_rs,
     w_ss,
     w_rs,
     z_ss,
@@ -91,18 +101,35 @@
     diag = (wide_of(1 - y, z, 1 - c), n)
     zpeer = [(wide_of(y, wrap(z + k, 8), c), n) for k in range(1, 8)]
 
-    def w_index(r):
-        return lax.rem(e + r + 16, 16)
-
-    def w_peer(r):
-        d = w_index(r)
-        return (wide_of(lax.div(d, 8), z, c), lax.rem(d, 8))
-
-    def n_peer(k):
-        return (w, lax.rem(n + k, 8))
+    x = lax.rem(n, 4)
+    yh = lax.div(n, 4)
+    v = 2 * y + yh
+
+    def x_peer(k, cc):
+        return (wide_of(y, z, cc), yh * 4 + wrap(x + k, 4))
+
+    def y_peer(k, cc):
+        far = wrap(v + k, 4)
+        return (wide_of(lax.div(far, 2), z, cc), lax.rem(far, 2) * 4 + x)
+
+    line_peer = (x_peer, y_peer)
+    line_at = (x, v)
+
+    loads = [
+        pltpu.make_async_copy(src, dst, in_s.at[i])
+        for i, (src, dst) in enumerate(
+            ((route_hbm, route_ref), (mol_hbm, mol_ref), (act_hbm, act_ref))
+        )
+    ]
+    for cp in loads:
+        cp.start()
 
     barrier = pltpu.get_barrier_semaphore()
-    partners = zpeer + [sib, diag] + [w_peer(r) for r in range(1, 16)]
+    partners = zpeer + [sib]
+    for peer in line_peer:
+        partners += [peer(k, cc) for k in (1, 2, 3) for cc in (c, 1 - c)]
+    for k in (1, 2, 3):
+        partners.append((w, (1 - yh) * 4 + wrap(x + k, 4)))
     for dev in partners:
         pl.semaphore_signal(barrier, inc=1, device_id=dev, device_id_type=MESH)
 
@@ -132,7 +159,9 @@
 
         loop(ROWS // 32, body)
 
+    loads[0].wait()
     normalise(route_ref, ring_r, cross_r)
+    loads[1].wait()
     normalise(mol_ref, ring_m, cross_m)
     t_own = jnp.concatenate(
         [target_ref[...].astype(F32), jnp.zeros((1, 256 - ROWS), F32)], axis=1
@@ -191,43 +220,95 @@
     def cross_wait(a, i):
         cross_copy(a, i, (b_across, b_sib, b_diag)[i], sib).wait_recv()
 
-    for k in range(1, 8):
-        send(tring.at[z], tring.at[z], t_ss.at[k - 1], t_rs.at[k - 1], zpeer[k - 1])
-    for i, dev in enumerate((sib, across, diag)):
+    def target_ring():
+        for k in range(1, 8):
+            send(tring.at[z], tring.at[z], t_ss.at[k - 1], t_rs.at[k - 1], zpeer[k - 1])
+
+    def target_ring_wait():
+        for k in range(1, 8):
+            at = tring.at[wrap(z - k, 8)]
+            remote(at, at, t_ss.at[k - 1], t_rs.at[k - 1], sib).wait_recv()
+
+    ring_open(0)
+    cross_send(0, 0)
+    for i, dev in enumerate((across, sib, diag)):
         send(tcross.at[q], tcross.at[q], t_ss.at[7 + i], t_rs.at[7 + i], dev)
-
-    cross_send(0, 0)
-    ring_open(0)
     cross_send(0, 1)
 
+    loads[2].wait()
     for t in range(16):
         tile = act_ref[:, 128 * t : 128 * t + 128].astype(F32)
         act_t[128 * t : 128 * t + 128, :] = tile.T
 
     def order(j):
-        yy, nn = lax.div(j, 8), lax.rem(j, 8)
+        vv, xx = lax.div(j, 4), lax.rem(j, 4)
+        yy, nn = lax.div(vv, 2), lax.rem(vv, 2) * 4 + xx
         for h in (0, 1):
-            parts = [
+            rows = [
                 act_t[pl.ds(pl.multiple_of(1024 * yy + 128 * zz + 64 * h + 8 * nn, 8), 8), :]
                 for zz in range(8)
             ]
-            act_own[h, pl.ds(pl.multiple_of(j * 64, 64), 64), :] = jnp.concatenate(
-                parts, axis=0
-            ).astype(BF16)
+            act_own[h, vv, xx] = jnp.concatenate(rows, axis=0).astype(BF16)
 
     loop(16, order)
-    send(act_own.at[1 - c], act_sib, mis_ss.at[0], mis_rs.at[0], sib)
+
+    acts = (act_x, act_y)
+    molds = (mold_x, mold_y)
+
+    def act_part(l, h, at):
+        return act_own.at[h, :, at] if l == 0 else act_own.at[h, at]
+
+    own_acts = [
+        pltpu.make_async_copy(act_part(l, c, line_at[l]), acts[l].at[line_at[l], c], in_s.at[3 + l])
+        for l in (0, 1)
+    ]
+    for cp in own_acts:
+        cp.start()
+
+    def act_send(l):
+        here = acts[l].at[line_at[l], c]
+        for k in range(4):
+            for o in (0, 1):
+                if k + o > 0:
+                    i = l * 8 + k * 2 + o
+                    cc = c if o == 0 else 1 - c
+                    src = act_part(l, cc, wrap(line_at[l] + k, 4))
+                    send(src, here, act_ss.at[i], act_rs.at[i], line_peer[l](k, cc))
+
+    def act_wait():
+        for cp in own_acts:
+            cp.wait()
+        for l in (0, 1):
+            for k in range(4):
+                for o in (0, 1):
+                    if k + o > 0:
+                        i = l * 8 + k * 2 + o
+                        cc = c if o == 0 else 1 - c
+                        dst = acts[l].at[wrap(line_at[l] - k, 4), cc]
+                        remote(dst, dst, act_ss.at[i], act_rs.at[i], sib).wait_recv()
+
+    def mold_copy(l, k, o, at, dev):
+        i = l * 8 + k * 2 + o
+        return remote(at, at, mold_ss.at[i], mold_rs.at[i], dev)
+
+    def mold_send(l, k, o):
+        if o == 0:
+            at, dev = molds[l].at[line_at[l], c], line_peer[l](k, c)
+        else:
+            at, dev = molds[l].at[wrap(line_at[l] - k, 4), c], sib
+        cp = mold_copy(l, k, o, at, dev)
+        cp.start()
+        sent.append(cp)
+
+    def mold_wait(l, k, o):
+        at = molds[l].at[wrap(line_at[l] - k, 4), c if o == 0 else 1 - c]
+        mold_copy(l, k, o, at, sib).wait_recv()
 
     advance(0, 0)
     cross_wait(0, 0)
     cross_send(0, 2)
 
-    for k in range(1, 8):
-        slot = wrap(z - k, 8)
-        remote(
-            tring.at[slot], tring.at[slot], t_ss.at[k - 1], t_rs.at[k - 1], sib
-        ).wait_recv()
-    for i, slot in enumerate((2 * y + 1 - c, 2 * (1 - y) + c, 2 * (1 - y) + 1 - c)):
+    for i, slot in enumerate((2 * (1 - y) + c, 2 * y + 1 - c, 2 * (1 - y) + 1 - c)):
         remote(
             tcross.at[slot], tcross.at[slot], t_ss.at[7 + i], t_rs.at[7 + i], sib
         ).wait_recv()
@@ -246,32 +327,42 @@
     seed = seed_ref[0]
     parts = (part_m, part_r)
 
-    def pairs(a, slot, first):
-        def body(b):
-            rows = pl.ds(pl.multiple_of(b * PAIR, PAIR), PAIR)
-            right = rings[a][slot]
-            sharp = jnp.exp(jnp.full((1, ROWS), sharp_ref[0], F32))
-            s = lax.dot_general(crosses[a][rows, :], right, NT, preferred_element_type=F32)
+    def pairs(a, slot, first=False):
+        right = rings[a][slot]
+        sharp = jnp.exp(jnp.full((1, ROWS), sharp_ref[0], F32))
+        blocks = [pl.ds(i * ROWS, ROWS) for i in range(4)]
+
+        def grads(i, s):
             if a == 0:
-                base = wide_of(y, slot, c) * ROWS
-                ids = lax.broadcasted_iota(jnp.int32, (1, ROWS), 1) + base
-                match = tcol[rows, 0:1] == ids.astype(F32)
+                ids = lax.broadcasted_iota(jnp.int32, (1, ROWS), 1) + wide_of(y, slot, c) * ROWS
+                match = tcol[blocks[i], 0:1] == ids.astype(F32)
             else:
-                base = wide_of(b, z, 0) * ROWS
-                ids = lax.broadcasted_iota(jnp.int32, (PAIR, 1), 0) + base
+                base = wide_of(i // 2, z, i % 2) * ROWS
+                ids = lax.broadcasted_iota(jnp.int32, (ROWS, 1), 0) + base
                 match = ids.astype(F32) == tring[slot, 0:1, 0:ROWS]
             g = jax.nn.sigmoid(s * sharp + shift) - jnp.where(match, 1.0, 0.0)
-            g = (seed * g).astype(BF16)
+            return (seed * g).astype(BF16)
+
+        scores = [
+            lax.dot_general(crosses[a][b, :], right, NT, preferred_element_type=F32)
+            for b in blocks
+        ]
+        gs = [grads(i, s) for i, s in enumerate(scores)]
+        for b, g in zip(blocks, gs):
             out = lax.dot_general(g, right, NN, preferred_element_type=F32)
             if first:
-                parts[a][rows, :] = out
+                parts[a][b, :] = out
             else:
-                parts[a][rows, :] += out
-
-        loop(2, body)
+                parts[a][b, :] += out
+
+    def pairs_left(a, k):
+        pairs(a, wrap(z - k, 8))
+
+    def pairs_right(a, k):
+        pairs(a, wrap(z + k, 8))
 
     def pairs_at(a, k):
-        loop(2, lambda i: pairs(a, wrap(z + (2 * i - 1) * k, 8), False))
+        loop(2, lambda i: pairs(a, wrap(z + (2 * i - 1) * k, 8)))
 
     def reduce_open(a):
         send(parts[a].at[b_diag], sib_in.at[a, 0], red_ss.at[a * 4], red_rs.at[a * 4], sib)
@@ -281,7 +372,12 @@
         dst = (sib_in.at[a, 0], sib_in.at[a, 1], y_in.at[a], a_in.at[a])[i]
         remote(dst, dst, red_ss.at[a * 4 + i], red_rs.at[a * 4 + i], sib).wait_recv()
 
+    def diagonal(i):
+        row = lax.broadcasted_iota(jnp.int32, (32, ROWS), 0) + i * 32
+        return row == lax.broadcasted_iota(jnp.int32, (32, ROWS), 1)
+
     def reduce_across(a):
+        a_out[a] = jnp.zeros((8, ROWS), F32)
         reduce_wait(a, 0)
 
         def body(i):
@@ -291,7 +387,8 @@
             unit = crosses[a][far, :].astype(F32)
             along = jnp.sum(total * unit, -1, keepdims=True)
             y_out[a, rows, :] = (total - along * unit).astype(BF16)
-            a_out[a, rows, :] = jnp.broadcast_to(along, (32, 128))
+            spread = jnp.sum(jnp.where(diagonal(i), along, 0.0), 0, keepdims=True)
+            a_out[a] += jnp.broadcast_to(spread, (8, ROWS))
 
         loop(ROWS // 32, body)
         send(y_out.at[a], y_in.at[a], red_ss.at[a * 4 + 2], red_rs.at[a * 4 + 2], across)
@@ -307,7 +404,8 @@
             own = pl.ds(pl.multiple_of(q * ROWS + i * 32, 32), 32)
             sharp = jnp.exp(jnp.full((32, 1), sharp_ref[0], F32))
             total = parts[a][own, :] + sib_in[a, 1, rows, :] + y_in[a, rows, :].astype(F32)
-            total = total + a_in[a, rows, 0:1] * crosses[a][own, :].astype(F32)
+            along = jnp.sum(jnp.where(diagonal(i), a_in[a, 0:1, :], 0.0), -1, keepdims=True)
+            total = total + along * crosses[a][own, :].astype(F32)
             v = raw[rows, :].astype(F32)
             inv = 1.0 / jnp.sqrt(jnp.sum(v * v, -1, keepdims=True) + 1e-06)
             unit = v * inv
@@ -316,96 +414,136 @@
 
         loop(ROWS // 32, body)
 
-    pairs(0, z, True)
-    pairs_at(0, 1)
-    advance(0, 1)
     cross_send(1, 0)
     cross_send(1, 1)
-    pairs_at(0, 2)
-    advance(0, 2)
+    target_ring()
+    act_send(0)
+    act_send(1)
+    pairs(0, z, True)
+    pairs_left(0, 1)
+    advance(0, 1, (0,))
+    pairs_right(0, 1)
+    advance(0, 1, (1,))
+    pairs_left(0, 2)
+    advance(0, 2, (0,))
+    pairs_right(0, 2)
+    advance(0, 2, (1,))
     ring_open(1)
-    pairs_at(0, 3)
     cross_wait(1, 0)
     cross_send(1, 2)
+    pairs_at(0, 3)
     advance(0, 3)
-    pairs(0, wrap(z + 4, 8), False)
+    pairs_right(0, 4)
 
     reduce_open(0)
+    cross_wait(1, 1)
+    cross_wait(1, 2)
+    target_ring_wait()
     advance(1, 0, (0,))
     reduce_across(0)
-    cross_wait(1, 1)
-    cross_wait(1, 2)
     pairs(1, z, True)
     advance(1, 0, (1,))
-    pairs_at(1, 1)
+    pairs_left(1, 1)
     advance(1, 1, (0,))
+    pairs_right(1, 1)
+    advance(1, 1, (1,))
 
     def put_mold(i, value):
-        mold[c, pl.ds(pl.multiple_of(i * 32, 32), 32), :] = value
+        rows = pl.ds(pl.multiple_of(i * 32, 32), 32)
+        mold_x[x, c, rows, :] = value[:, : D // 2]
+        mold_y[v, c, rows, :] = value[:, D // 2 :]
 
     reduce_close(0, mol_ref, put_mold)
-    send(mold.at[c], mold.at[c], mis_ss.at[1], mis_rs.at[1], sib)
-    advance(1, 1, (1,))
-    remote(act_sib, act_sib, mis_ss.at[0], mis_rs.at[0], sib).wait_recv()
-    remote(mold.at[1 - c], mold.at[1 - c], mis_ss.at[1], mis_rs.at[1], sib).wait_recv()
+    for k in (2, 1, 3):
+        for l in (0, 1):
+            mold_send(l, k, 0)
+    for l in (0, 1):
+        mold_send(l, 0, 1)
+    pairs_left(1, 2)
+    advance(1, 2, (0,))
+    pairs_right(1, 2)
+    advance(1, 2, (1,))
+    for k in (1, 3, 2):
+        for l in (0, 1):
+            mold_wait(l, k, 0)
+            mold_send(l, k, 1)
+    pairs_left(1, 3)
+    act_wait()
+    for k in (0, 1, 3, 2):
+        for l in (0, 1):
+            mold_wait(l, k, 1)
 
     def weight(i):
         cols = pl.ds(pl.multiple_of(i * 256, 256), 256)
-        prod = lax.dot_general(act_own[c], mold[c, :, cols], NN, preferred_element_type=F32)
-        prod += lax.dot_general(act_sib[...], mold[1 - c, :, cols], NN, preferred_element_type=F32)
-        wsend[:, :, cols] = prod.astype(BF16).reshape(16, 64, 256)
-
-    loop(4, weight)
-    for r in range(1, 16):
-        send(wsend.at[w_index(r)], wrecv.at[e], w_ss.at[r - 1], w_rs.at[r - 1], w_peer(r))
-
-    advance(1, 2, (0,))
-    pairs_at(1, 2)
-    advance(1, 2, (1,))
-    pairs_at(1, 3)
+        for l in (0, 1):
+            total = jnp.zeros((256, 256), F32)
+            for p in range(4):
+                for cc in (0, 1):
+                    total += lax.dot_general(
+                        acts[l][p, cc].reshape(256, ROWS),
+                        molds[l][p, cc, :, cols],
+                        NN,
+                        preferred_element_type=F32,
+                    )
+            total = total.reshape(4, 64, 256)
+            prod[l, :, :, cols] = total
+            wsend[l, :, :, cols] = total.astype(BF16)
+
+    loop(2, weight)
+    for k in (2, 1, 3):
+        for l in (0, 1):
+            m = 1 - l
+            i = l * 3 + k - 1
+            src = wsend.at[l, wrap(line_at[m] + k, 4)]
+            send(src, wrecv.at[l, line_at[m]], w_ss.at[i], w_rs.at[i], line_peer[m](k, c))
+
+    pairs_right(1, 3)
     advance(1, 3)
-    pairs(1, wrap(z + 4, 8), False)
+    pairs_right(1, 4)
     reduce_open(1)
     reduce_across(1)
 
-    for r in range(1, 16):
-        slot = w_index(-r)
-        remote(
-            wrecv.at[slot], wrecv.at[slot], w_ss.at[r - 1], w_rs.at[r - 1], sib
-        ).wait_recv()
+    for l in (0, 1):
+        for k in (1, 2, 3):
+            i = l * 3 + k - 1
+            at = wrecv.at[l, wrap(line_at[1 - l] - k, 4)]
+            remote(at, at, w_ss.at[i], w_rs.at[i], sib).wait_recv()
 
     def gather_sum(i):
         rows = pl.ds(pl.multiple_of(i * 16, 16), 16)
-        total = wsend[e, rows, :].astype(F32)
-        for r in range(1, 16):
-            total += wrecv[w_index(-r), rows, :].astype(F32)
-        zsend[rows, :] = total
+        halves = []
+        for l in (0, 1):
+            total = prod[l, line_at[1 - l], rows, :]
+            for k in (1, 2, 3):
+                total += wrecv[l, wrap(line_at[1 - l] - k, 4), rows, :].astype(F32)
+            halves.append(total)
+        for o in (0, 1):
+            both = jnp.concatenate([total[8 * o : 8 * o + 8, :] for total in halves], axis=0)
+            zown[2 * i + o] = both
+            zsend[2 * i + o] = both.astype(BF16)
 
     loop(4, gather_sum)
     for k in range(1, 8):
-        src = zsend.at[pl.ds(pl.multiple_of(wrap(z + k, 8) * 8, 8), 8)]
+        src = zsend.at[wrap(z + k, 8)]
         send(src, zrecv.at[z], z_ss.at[k - 1], z_rs.at[k - 1], zpeer[k - 1])
+    total = zown[z]
+    for k in range(1, 8):
+        at = zrecv.at[wrap(z - k, 8)]
+        remote(at, at, z_ss.at[k - 1], z_rs.at[k - 1], sib).wait_recv()
+        total += zrecv[wrap(z - k, 8)].astype(F32)
+    total = jnp.concatenate([total[0:8, :], total[8:16, :]], axis=1)
+    gath[n] = total
+    for k in (4, 2, 6, 1, 3, 5, 7):
+        dev = (w, lax.rem(n + k, 8))
+        send(gath.at[n], gath.at[n], g_ss.at[k - 1], g_rs.at[k - 1], dev)
 
     def put_route(i, value):
         route_out[pl.ds(pl.multiple_of(i * 32, 32), 32), :] = value
 
     reduce_close(1, route_ref, put_route)
-
-    total = zsend[pl.ds(pl.multiple_of(z * 8, 8), 8), :]
     for k in range(1, 8):
-        slot = wrap(z - k, 8)
-        remote(
-            zrecv.at[slot], zrecv.at[slot], z_ss.at[k - 1], z_rs.at[k - 1], sib
-        ).wait_recv()
-        total += zrecv[slot]
-    gath[n] = total
-    for k in range(1, 8):
-        send(gath.at[n], gath.at[n], g_ss.at[k - 1], g_rs.at[k - 1], n_peer(k))
-    for k in range(1, 8):
-        slot = wrap(n - k, 8)
-        remote(
-            gath.at[slot], gath.at[slot], g_ss.at[k - 1], g_rs.at[k - 1], sib
-        ).wait_recv()
+        at = gath.at[lax.rem(n - k + 8, 8)]
+        remote(at, at, g_ss.at[k - 1], g_rs.at[k - 1], sib).wait_recv()
     weight_out[...] = gath[...].reshape(64, D)
     for cp in sent:
         cp.wait_send()
@@ -421,6 +559,7 @@
     objective_seed,
 ):
     vmem = pl.BlockSpec(memory_space=pltpu.VMEM)
+    hbm = pl.BlockSpec(memory_space=pltpu.HBM)
     smem = pl.BlockSpec(memory_space=pltpu.SMEM)
     dma = pltpu.SemaphoreType.DMA
     weight_grad, route_grad = pl.pallas_call(
@@ -429,9 +568,12 @@
             jax.ShapeDtypeStruct((64, D), F32),
             jax.ShapeDtypeStruct((ROWS, D), BF16),
         ),
-        in_specs=[vmem] * 4 + [smem] * 3,
+        in_specs=[hbm] * 3 + [vmem] + [smem] * 3,
         out_specs=(vmem, vmem),
         scratch_shapes=[
+            pltpu.VMEM((ROWS, FF), BF16),
+            pltpu.VMEM((ROWS, D), BF16),
+            pltpu.VMEM((ROWS, D), BF16),
             pltpu.VMEM((8, ROWS, D), BF16),
             pltpu.VMEM((8, ROWS, D), BF16),
             pltpu.VMEM((4 * ROWS, D), BF16),
@@ -444,16 +586,20 @@
             pltpu.VMEM((2, 2, ROWS, D), F32),
             pltpu.VMEM((2, ROWS, D), BF16),
             pltpu.VMEM((2, ROWS, D), BF16),
-            pltpu.VMEM((2, ROWS, 128), F32),
-            pltpu.VMEM((2, ROWS, 128), F32),
+            pltpu.VMEM((2, 8, ROWS), F32),
+            pltpu.VMEM((2, 8, ROWS), F32),
             pltpu.VMEM((FF, ROWS), F32),
-            pltpu.VMEM((2, FF // 2, ROWS), BF16),
-            pltpu.VMEM((FF // 2, ROWS), BF16),
-            pltpu.VMEM((2, ROWS, D), BF16),
-            pltpu.VMEM((16, 64, D), BF16),
-            pltpu.VMEM((16, 64, D), BF16),
-            pltpu.VMEM((64, D), F32),
-            pltpu.VMEM((8, 8, D), F32),
+            pltpu.VMEM((2, 4, 4, 64, ROWS), BF16),
+            pltpu.VMEM((4, 2, 4, 64, ROWS), BF16),
+            pltpu.VMEM((4, 2, 4, 64, ROWS), BF16),
+            pltpu.VMEM((4, 2, ROWS, D // 2), BF16),
+            pltpu.VMEM((4, 2, ROWS, D // 2), BF16),
+            pltpu.VMEM((2, 4, 64, D // 2), F32),
+            pltpu.VMEM((2, 4, 64, D // 2), BF16),
+            pltpu.VMEM((2, 4, 64, D // 2), BF16),
+            pltpu.VMEM((8, 16, D // 2), F32),
+            pltpu.VMEM((8, 16, D // 2), BF16),
+            pltpu.VMEM((8, 16, D // 2), BF16),
             pltpu.VMEM((8, 8, D), F32),
             dma((32,)),
             dma((32,)),
@@ -463,17 +609,20 @@
             dma((10,)),
             dma((8,)),
             dma((8,)),
-            dma((2,)),
-            dma((2,)),
-            dma((15,)),
-            dma((15,)),
+            dma((5,)),
+            dma((16,)),
+            dma((16,)),
+            dma((16,)),
+            dma((16,)),
+            dma((6,)),
+            dma((6,)),
             dma((7,)),
             dma((7,)),
             dma((7,)),
             dma((7,)),
         ],
         compiler_params=pltpu.CompilerParams(
-            collective_id=0, has_side_effects=True, vmem_limit_bytes=48 * 1024 * 1024
+            collective_id=0, has_side_effects=True, vmem_limit_bytes=60 * 1024 * 1024
         ),
         name="contrastive_backward",
     )(

time: 119 us -> 91.8 us (0.77)
  Pallas kernels: 110 us -> 86.3 us
  local copies, waits for them, and re-layouts: 5.13 us -> 2.45 us
    pallas_call x1, Pallas kernels: 110 us -> 86.3 us  [local(): pl.pallas_call(kernel, out_shape=(jax.ShapeDtypeStruct((64, D), F32), jax...]
    unnamed x10 -> x4, local copies, waits for them, and re-layouts: 5.13 us -> 2.45 us
where the time goes in v2:
time: 91.8 us; the launch traced here: 91.3 us
  Pallas kernels  86.3 us (94%)
  between operations  2.59 us (3%)
  local copies, waits for them, and re-layouts  2.45 us (3%)
    pallas_call x1, Pallas kernels, local(): pl.pallas_call(kernel, out_shape=(jax.ShapeDtypeStruct((64, D), F32), jax...  86.3 us
    unnamed x4, local copies, waits for them, and re-layouts  2.45 us

profile of v2, /device:TPU:2, one launch (start us, length us, event | category | flops | bytes accessed | tf_op | source)
XLA Modules:
  0.0 91.3 jit_solution(700778031221888042)
XLA Ops:
  2.6 86.3 %contrastive_backward.1 = (f32[64,1024]{1,0:T(8,128)}, bf16[160,1024]{1,0:T(8,128)(2,1)}) custom-call(bf16[160,2048]{1,0:T(8,128)(2,1)} %bitcast.4, bf16[160,1024]{1,0:T(8,128)(2,1)} %bitcast.6, bf16[160,1024]{1,0:T(8,128)(2,1)} %bitcast.7, s32[1,160]{1,0:T(1,128)} %target_ref.1, f32[1]{0:T(128)S(6)} %copy.11.sharp_ref, f32[1]{0:T(128)S(6)} %copy.12.shift_ref, ...), custom_call_target="tpu_custom_call" | custom-call | tf_op jit(solution)/shard_map/contrastive_backward/pallas_call | solution.py:565
  88.9 0.0 copy-start
  88.9 1.7 %copy.14 = f32[64,1024]{1,0:T(8,128)} copy(f32[64,1024]{1,0:T(8,128)} %get-tuple-element.8) | data formatting | bytes 524288
  90.6 0.0 copy-done
  90.6 0.7 copy.15
Async XLA Ops:
  88.9 1.7 %copy-start = (bf16[160,1024]{1,0:T(8,128)(2,1)S(1)}, bf16[160,1024]{1,0:T(8,128)(2,1)}, u32[]{:S(2)}) copy-start(bf16[160,1024]{1,0:T(8,128)(2,1)} %get-tuple-element.5) | copy-start | bytes 983044

commit v3 on v2

--- a/solution.py
+++ b/solution.py
@@ -6,7 +6,8 @@
 from jax.sharding import PartitionSpec as P
 
 ROWS = 160
-HALF = 80
+PIECES = ((0, 48), (48, 32), (80, 48), (128, 32))
+CHUNKS = ((0, 64), (64, 96))
 D = 1024
 FF = 2048
 PAIR = 2 * ROWS
@@ -161,12 +162,9 @@
 
     loads[0].wait()
     normalise(route_ref, ring_r, cross_r)
-    loads[1].wait()
-    normalise(mol_ref, ring_m, cross_m)
     t_own = jnp.concatenate(
         [target_ref[...].astype(F32), jnp.zeros((1, 256 - ROWS), F32)], axis=1
     )
-    t_own = jnp.broadcast_to(t_own, (8, 256))
     tring[z] = t_own
     tcross[q] = t_own
 
@@ -175,11 +173,11 @@
     rings = (ring_r, ring_m)
 
     def exists(d, k, h):
-        return k < 3 or (k == 3 and h == d)
+        return k < 3 or (k == 3 and h // 2 == d)
 
     def ring_copy(a, d, k, h, slot):
-        i = ((a * 2 + d) * 4 + k) * 2 + h
-        part = rings[a].at[slot, pl.ds(h * HALF, HALF)]
+        i = ((a * 2 + d) * 4 + k) * 4 + h
+        part = rings[a].at[slot, pl.ds(*PIECES[h])]
         dev = zpeer[0] if d == 0 else zpeer[6]
         return remote(part, part, ring_ss.at[i], ring_rs.at[i], dev)
 
@@ -191,18 +189,21 @@
     def ring_wait(a, d, k, h):
         ring_copy(a, d, k, h, wrap(z - 1 - k, 8) if d == 0 else wrap(z + 1 + k, 8)).wait_recv()
 
-    def advance(a, k, pieces=(0, 1)):
-        for h in pieces:
+    order_of = ((0, 1, 2, 3), (2, 3, 0, 1))
+
+    def advance(a, k, places=(0, 1, 2, 3)):
+        for o in places:
             for d in (0, 1):
+                h = order_of[d][o]
                 if exists(d, k, h):
                     ring_wait(a, d, k, h)
                     if exists(d, k + 1, h):
                         ring_send(a, d, k + 1, h)
 
     def ring_open(a):
-        for h in (0, 1):
+        for o in range(4):
             for d in (0, 1):
-                ring_send(a, d, 0, h)
+                ring_send(a, d, 0, order_of[d][o])
 
     crosses = (cross_m, cross_r)
     b_own, b_sib = block(q), block(2 * y + 1 - c)
@@ -230,6 +231,8 @@
             remote(at, at, t_ss.at[k - 1], t_rs.at[k - 1], sib).wait_recv()
 
     ring_open(0)
+    loads[1].wait()
+    normalise(mol_ref, ring_m, cross_m)
     cross_send(0, 0)
     for i, dev in enumerate((across, sib, diag)):
         send(tcross.at[q], tcross.at[q], t_ss.at[7 + i], t_rs.at[7 + i], dev)
@@ -287,22 +290,35 @@
                         dst = acts[l].at[wrap(line_at[l] - k, 4), cc]
                         remote(dst, dst, act_ss.at[i], act_rs.at[i], sib).wait_recv()
 
-    def mold_copy(l, k, o, at, dev):
-        i = l * 8 + k * 2 + o
+    def mold_copy(l, k, o, j, p, cc, dev):
+        i = ((l * 4 + k) * 2 + o) * 2 + j
+        at = molds[l].at[p, cc, pl.ds(*CHUNKS[j])]
         return remote(at, at, mold_ss.at[i], mold_rs.at[i], dev)
 
-    def mold_send(l, k, o):
+    def mold_send(l, k, o, j):
         if o == 0:
-            at, dev = molds[l].at[line_at[l], c], line_peer[l](k, c)
+            cp = mold_copy(l, k, o, j, line_at[l], c, line_peer[l](k, c))
         else:
-            at, dev = molds[l].at[wrap(line_at[l] - k, 4), c], sib
-        cp = mold_copy(l, k, o, at, dev)
+            cp = mold_copy(l, k, o, j, wrap(line_at[l] - k, 4), c, sib)
         cp.start()
         sent.append(cp)
 
-    def mold_wait(l, k, o):
-        at = molds[l].at[wrap(line_at[l] - k, 4), c if o == 0 else 1 - c]
-        mold_copy(l, k, o, at, sib).wait_recv()
+    def mold_wait(l, k, o, j):
+        cc = c if o == 0 else 1 - c
+        mold_copy(l, k, o, j, wrap(line_at[l] - k, 4), cc, sib).wait_recv()
+
+    def mold_round(j):
+        for k in (2, 1, 3):
+            for l in (0, 1):
+                mold_send(l, k, 0, j)
+        for l in (0, 1):
+            mold_send(l, 0, 1, j)
+
+    def mold_pass(j):
+        for k in (1, 3, 2):
+            for l in (0, 1):
+                mold_wait(l, k, 0, j)
+                mold_send(l, k, 1, j)
 
     advance(0, 0)
     cross_wait(0, 0)
@@ -364,21 +380,41 @@
     def pairs_at(a, k):
         loop(2, lambda i: pairs(a, wrap(z + (2 * i - 1) * k, 8)))
 
+    def reduce_copy(a, i, j):
+        rows = pl.ds(*CHUNKS[j])
+        dev = sib
+        if i < 2:
+            q_ = 2 * (1 - y) + 1 - c if i == 0 else 2 * y + 1 - c
+            here = pl.ds(pl.multiple_of(q_ * ROWS + CHUNKS[j][0], 32), CHUNKS[j][1])
+            src, dst = parts[a].at[here], sib_in.at[a, i, rows]
+        elif i == 2:
+            src, dst, dev = y_out.at[a, rows], y_in.at[a, rows], across
+        else:
+            src, dst, dev = a_out.at[a, j], a_in.at[a, j], across
+        i = (a * 4 + i) * 2 + j
+        return remote(src, dst, red_ss.at[i], red_rs.at[i], dev)
+
+    def reduce_send(a, i, j):
+        cp = reduce_copy(a, i, j)
+        cp.start()
+        sent.append(cp)
+
     def reduce_open(a):
-        send(parts[a].at[b_diag], sib_in.at[a, 0], red_ss.at[a * 4], red_rs.at[a * 4], sib)
-        send(parts[a].at[b_sib], sib_in.at[a, 1], red_ss.at[a * 4 + 1], red_rs.at[a * 4 + 1], sib)
-
-    def reduce_wait(a, i):
-        dst = (sib_in.at[a, 0], sib_in.at[a, 1], y_in.at[a], a_in.at[a])[i]
-        remote(dst, dst, red_ss.at[a * 4 + i], red_rs.at[a * 4 + i], sib).wait_recv()
+        for i in (0, 1):
+            for j in (0, 1):
+                reduce_send(a, i, j)
 
     def diagonal(i):
         row = lax.broadcasted_iota(jnp.int32, (32, ROWS), 0) + i * 32
         return row == lax.broadcasted_iota(jnp.int32, (32, ROWS), 1)
 
-    def reduce_across(a):
-        a_out[a] = jnp.zeros((8, ROWS), F32)
-        reduce_wait(a, 0)
+    def blocks_of(j, body):
+        first, size = CHUNKS[j]
+        loop(size // 32, lambda i: body(i + first // 32))
+
+    def reduce_across(a, j):
+        a_out[a, j] = jnp.zeros((8, ROWS), F32)
+        reduce_copy(a, 0, j).wait_recv()
 
         def body(i):
             rows = pl.ds(pl.multiple_of(i * 32, 32), 32)
@@ -388,31 +424,37 @@
             along = jnp.sum(total * unit, -1, keepdims=True)
             y_out[a, rows, :] = (total - along * unit).astype(BF16)
             spread = jnp.sum(jnp.where(diagonal(i), along, 0.0), 0, keepdims=True)
-            a_out[a] += jnp.broadcast_to(spread, (8, ROWS))
-
-        loop(ROWS // 32, body)
-        send(y_out.at[a], y_in.at[a], red_ss.at[a * 4 + 2], red_rs.at[a * 4 + 2], across)
-        send(a_out.at[a], a_in.at[a], red_ss.at[a * 4 + 3], red_rs.at[a * 4 + 3], across)
-
-    def reduce_close(a, raw, put):
-        reduce_wait(a, 1)
-        reduce_wait(a, 2)
-        reduce_wait(a, 3)
+            a_out[a, j] += jnp.broadcast_to(spread, (8, ROWS))
+
+        blocks_of(j, body)
+        reduce_send(a, 2, j)
+        reduce_send(a, 3, j)
+
+    def reduce_close(a, j, raw, put):
+        for i in (1, 2, 3):
+            reduce_copy(a, i, j).wait_recv()
 
         def body(i):
             rows = pl.ds(pl.multiple_of(i * 32, 32), 32)
             own = pl.ds(pl.multiple_of(q * ROWS + i * 32, 32), 32)
             sharp = jnp.exp(jnp.full((32, 1), sharp_ref[0], F32))
             total = parts[a][own, :] + sib_in[a, 1, rows, :] + y_in[a, rows, :].astype(F32)
-            along = jnp.sum(jnp.where(diagonal(i), a_in[a, 0:1, :], 0.0), -1, keepdims=True)
+            along = jnp.sum(jnp.where(diagonal(i), a_in[a, j, 0:1, :], 0.0), -1, keepdims=True)
             total = total + along * crosses[a][own, :].astype(F32)
             v = raw[rows, :].astype(F32)
             inv = 1.0 / jnp.sqrt(jnp.sum(v * v, -1, keepdims=True) + 1e-06)
             unit = v * inv
             along = jnp.sum(unit * total, -1, keepdims=True)
-            put(i, ((total - unit * along) * (inv * sharp)).astype(BF16))
-
-        loop(ROWS // 32, body)
+            put(rows, ((total - unit * along) * (inv * sharp)).astype(BF16))
+
+        blocks_of(j, body)
+
+    def put_mold(rows, value):
+        mold_x[x, c, rows, :] = value[:, : D // 2]
+        mold_y[v, c, rows, :] = value[:, D // 2 :]
+
+    def put_route(rows, value):
+        route_out[rows, :] = value
 
     cross_send(1, 0)
     cross_send(1, 1)
@@ -421,14 +463,14 @@
     act_send(1)
     pairs(0, z, True)
     pairs_left(0, 1)
-    advance(0, 1, (0,))
+    advance(0, 1, (0, 1))
     pairs_right(0, 1)
-    advance(0, 1, (1,))
+    advance(0, 1, (2, 3))
     pairs_left(0, 2)
-    advance(0, 2, (0,))
+    advance(0, 2, (0, 1))
+    ring_open(1)
     pairs_right(0, 2)
-    advance(0, 2, (1,))
-    ring_open(1)
+    advance(0, 2, (2, 3))
     cross_wait(1, 0)
     cross_send(1, 2)
     pairs_at(0, 3)
@@ -439,39 +481,29 @@
     cross_wait(1, 1)
     cross_wait(1, 2)
     target_ring_wait()
-    advance(1, 0, (0,))
-    reduce_across(0)
+    reduce_across(0, 0)
+    reduce_across(0, 1)
+    advance(1, 0, (0, 1))
     pairs(1, z, True)
-    advance(1, 0, (1,))
+    advance(1, 0, (2, 3))
     pairs_left(1, 1)
-    advance(1, 1, (0,))
+    reduce_close(0, 0, mol_ref, put_mold)
+    mold_round(0)
+    advance(1, 1, (0, 1))
+    reduce_close(0, 1, mol_ref, put_mold)
+    mold_round(1)
     pairs_right(1, 1)
-    advance(1, 1, (1,))
-
-    def put_mold(i, value):
-        rows = pl.ds(pl.multiple_of(i * 32, 32), 32)
-        mold_x[x, c, rows, :] = value[:, : D // 2]
-        mold_y[v, c, rows, :] = value[:, D // 2 :]
-
-    reduce_close(0, mol_ref, put_mold)
-    for k in (2, 1, 3):
-        for l in (0, 1):
-            mold_send(l, k, 0)
-    for l in (0, 1):
-        mold_send(l, 0, 1)
+    advance(1, 1, (2, 3))
+    mold_pass(0)
     pairs_left(1, 2)
-    advance(1, 2, (0,))
+    advance(1, 2, (0, 1))
+    mold_pass(1)
     pairs_right(1, 2)
-    advance(1, 2, (1,))
-    for k in (1, 3, 2):
-        for l in (0, 1):
-            mold_wait(l, k, 0)
-            mold_send(l, k, 1)
-    pairs_left(1, 3)
     act_wait()
-    for k in (0, 1, 3, 2):
-        for l in (0, 1):
-            mold_wait(l, k, 1)
+    for j in (0, 1):
+        for k in (0, 1, 3, 2):
+            for l in (0, 1):
+                mold_wait(l, k, 1, j)
 
     def weight(i):
         cols = pl.ds(pl.multiple_of(i * 256, 256), 256)
@@ -497,11 +529,12 @@
             src = wsend.at[l, wrap(line_at[m] + k, 4)]
             send(src, wrecv.at[l, line_at[m]], w_ss.at[i], w_rs.at[i], line_peer[m](k, c))
 
-    pairs_right(1, 3)
+    advance(1, 2, (2, 3))
+    pairs_at(1, 3)
     advance(1, 3)
     pairs_right(1, 4)
     reduce_open(1)
-    reduce_across(1)
+    reduce_across(1, 0)
 
     for l in (0, 1):
         for k in (1, 2, 3):
@@ -526,6 +559,7 @@
     for k in range(1, 8):
         src = zsend.at[wrap(z + k, 8)]
         send(src, zrecv.at[z], z_ss.at[k - 1], z_rs.at[k - 1], zpeer[k - 1])
+    reduce_across(1, 1)
     total = zown[z]
     for k in range(1, 8):
         at = zrecv.at[wrap(z - k, 8)]
@@ -537,10 +571,8 @@
         dev = (w, lax.rem(n + k, 8))
         send(gath.at[n], gath.at[n], g_ss.at[k - 1], g_rs.at[k - 1], dev)
 
-    def put_route(i, value):
-        route_out[pl.ds(pl.multiple_of(i * 32, 32), 32), :] = value
-
-    reduce_close(1, route_ref, put_route)
+    reduce_close(1, 0, route_ref, put_route)
+    reduce_close(1, 1, route_ref, put_route)
     for k in range(1, 8):
         at = gath.at[lax.rem(n - k + 8, 8)]
         remote(at, at, g_ss.at[k - 1], g_rs.at[k - 1], sib).wait_recv()
@@ -565,8 +597,8 @@
     weight_grad, route_grad = pl.pallas_call(
         kernel,
         out_shape=(
-            jax.ShapeDtypeStruct((64, D), F32),
-            jax.ShapeDtypeStruct((ROWS, D), BF16),
+            pltpu.VMEM((64, D), F32),
+            pltpu.VMEM((ROWS, D), BF16),
         ),
         in_specs=[hbm] * 3 + [vmem] + [smem] * 3,
         out_specs=(vmem, vmem),
@@ -578,16 +610,16 @@
             pltpu.VMEM((8, ROWS, D), BF16),
             pltpu.VMEM((4 * ROWS, D), BF16),
             pltpu.VMEM((4 * ROWS, D), BF16),
-            pltpu.VMEM((8, 8, 256), F32),
-            pltpu.VMEM((4, 8, 256), F32),
+            pltpu.VMEM((8, 1, 256), F32),
+            pltpu.VMEM((4, 1, 256), F32),
             pltpu.VMEM((4 * ROWS, 128), F32),
             pltpu.VMEM((4 * ROWS, D), F32),
             pltpu.VMEM((4 * ROWS, D), F32),
             pltpu.VMEM((2, 2, ROWS, D), F32),
             pltpu.VMEM((2, ROWS, D), BF16),
             pltpu.VMEM((2, ROWS, D), BF16),
-            pltpu.VMEM((2, 8, ROWS), F32),
-            pltpu.VMEM((2, 8, ROWS), F32),
+            pltpu.VMEM((2, 2, 8, ROWS), F32),
+            pltpu.VMEM((2, 2, 8, ROWS), F32),
             pltpu.VMEM((FF, ROWS), F32),
             pltpu.VMEM((2, 4, 4, 64, ROWS), BF16),
             pltpu.VMEM((4, 2, 4, 64, ROWS), BF16),
@@ -601,19 +633,19 @@
             pltpu.VMEM((8, 16, D // 2), BF16),
             pltpu.VMEM((8, 16, D // 2), BF16),
             pltpu.VMEM((8, 8, D), F32),
-            dma((32,)),
-            dma((32,)),
+            dma((64,)),
+            dma((64,)),
             dma((6,)),
             dma((6,)),
             dma((10,)),
             dma((10,)),
-            dma((8,)),
-            dma((8,)),
+            dma((16,)),
+            dma((16,)),
             dma((5,)),
             dma((16,)),
             dma((16,)),
-            dma((16,)),
-            dma((16,)),
+            dma((32,)),
+            dma((32,)),
             dma((6,)),
             dma((6,)),
             dma((7,)),

time: 91.8 us -> 85 us (0.926); the launches traced: 91.3 us -> 83.6 us
  Pallas kernels: 86.3 us -> 79.6 us
  local copies, waits for them, and re-layouts: 2.45 us -> 1.43 us
    pallas_call x1, Pallas kernels: 86.3 us -> 79.6 us  [local(): pl.pallas_call(kernel, out_shape=(pltpu.VMEM((64, D), F32), pltpu.VMEM((R...]
    unnamed x4 -> x2, local copies, waits for them, and re-layouts: 2.45 us -> 1.43 us
where the time goes in v3:
time: 85 us; the launch traced here: 83.6 us
  Pallas kernels  79.6 us (94%)
  between operations  2.58 us (3%)
  local copies, waits for them, and re-layouts  1.43 us (2%)
    pallas_call x1, Pallas kernels, local(): pl.pallas_call(kernel, out_shape=(pltpu.VMEM((64, D), F32), pltpu.VMEM((R...  79.6 us

profile of v3, /device:TPU:2, one launch (start us, length us, event | category | flops | bytes accessed | tf_op | source)
XLA Modules:
  0.0 83.6 jit_solution(11416346662945346637)
XLA Ops:
  2.6 79.6 %contrastive_backward.1 = (f32[64,1024]{1,0:T(8,128)S(1)}, bf16[160,1024]{1,0:T(8,128)(2,1)S(1)}) custom-call(bf16[160,2048]{1,0:T(8,128)(2,1)} %bitcast.5, bf16[160,1024]{1,0:T(8,128)(2,1)} %bitcast.6, bf16[160,1024]{1,0:T(8,128)(2,1)} %bitcast.7, s32[1,160]{1,0:T(1,128)} %target_ref.1, f32[1]{0:T(128)S(6)} %copy.13.sharp_ref, f32[1]{0:T(128)S(6)} %copy.14.shift_ref, ...), custom_call_target="tpu_custom_call" | custom-call | tf_op jit(solution)/shard_map/contrastive_backward/pallas_call | solution.py:597
  82.2 0.7 copy.11
  82.9 0.7 copy.12

commit v4 on v3

v4 whole, which is shorter than its diff:
```python
import jax
import jax.numpy as jnp
from jax import lax
from jax.experimental import pallas as pl
from jax.experimental.pallas import tpu as pltpu
from jax.sharding import PartitionSpec as P

ROWS = 160
PIECES = ((0, 48), (48, 32), (80, 48), (128, 32))
CHUNKS = ((0, 64), (64, 64), (128, 32))
D = 1024
FF = 2048
HALF = 80
F32 = jnp.float32
BF16 = jnp.bfloat16
MESH = pl.DeviceIdType.MESH
NT = (((1,), (1,)), ((), ()))
NN = (((1,), (0,)), ((), ()))
TN = (((0,), (0,)), ((), ()))


def wide_of(y, z, c):
    return y * 16 + z * 2 + c


def wrap(i, n):
    return lax.rem(i + n, n)


def loop(n, body):
    lax.fori_loop(0, n, lambda i, _: (body(i), 0)[1], 0)


def kernel(
    act_hbm,
    mol_hbm,
    route_hbm,
    target_ref,
    sharp_ref,
    shift_ref,
    seed_ref,
    weight_out,
    route_out,
    act_ref,
    mol_ref,
    route_ref,
    ring_r,
    cross_m,
    tcross,
    tcol,
    part_m,
    part_r,
    back_out,
    back_in,
    back_along,
    along_in,
    sib_in,
    y_out,
    y_in,
    a_out,
    a_in,
    act_t,
    act_own,
    act_x,
    act_y,
    mold_x,
    mold_y,
    prod,
    wsend,
    wrecv,
    zown,
    zsend,
    zrecv,
    gath,
    ring_ss,
    ring_rs,
    back_ss,
    back_rs,
    along_ss,
    along_rs,
    cross_ss,
    cross_rs,
    t_ss,
    t_rs,
    red_ss,
    red_rs,
    in_s,
    act_ss,
    act_rs,
    mold_ss,
    mold_rs,
    w_ss,
    w_rs,
    z_ss,
    z_rs,
    g_ss,
    g_rs,
):
    w = lax.axis_index("wide")
    n = lax.axis_index("narrow")
    y = lax.div(w, 16)
    z = lax.rem(lax.div(w, 2), 8)
    c = lax.rem(w, 2)
    q = 2 * y + c
    sib = (wide_of(y, z, 1 - c), n)
    across = (wide_of(1 - y, z, c), n)
    diag = (wide_of(1 - y, z, 1 - c), n)
    zpeer = [(wide_of(y, wrap(z + k, 8), c), n) for k in range(1, 8)]

    x = lax.rem(n, 4)
    yh = lax.div(n, 4)
    v = 2 * y + yh

    def x_peer(k, cc):
        return (wide_of(y, z, cc), yh * 4 + wrap(x + k, 4))

    def y_peer(k, cc):
        far = wrap(v + k, 4)
        return (wide_of(lax.div(far, 2), z, cc), lax.rem(far, 2) * 4 + x)

    line_peer = (x_peer, y_peer)
    line_at = (x, v)

    loads = [
        pltpu.make_async_copy(src, dst, in_s.at[i])
        for i, (src, dst) in enumerate(
            ((route_hbm, route_ref), (mol_hbm, mol_ref), (act_hbm, act_ref))
        )
    ]
    for cp in loads:
        cp.start()

    barrier = pltpu.get_barrier_semaphore()
    partners = zpeer + [sib]
    for peer in line_peer:
        partners += [peer(k, cc) for k in (1, 2, 3) for cc in (c, 1 - c)]
    for k in (1, 2, 3):
        partners.append((w, (1 - yh) * 4 + wrap(x + k, 4)))
    for dev in partners:
        pl.semaphore_signal(barrier, inc=1, device_id=dev, device_id_type=MESH)

    sent = []

    def remote(src, dst, ss, rs, dev):
        return pltpu.make_async_remote_copy(
            src_ref=src, dst_ref=dst, send_sem=ss, recv_sem=rs, device_id=dev, device_id_type=MESH
        )

    def send(*a):
        cp = remote(*a)
        cp.start()
        sent.append(cp)

    def block(q_):
        return pl.ds(pl.multiple_of(q_ * ROWS, ROWS), ROWS)

    def unit_rows(raw, rows):
        v = raw[rows, :].astype(F32)
        inv = 1.0 / jnp.sqrt(jnp.sum(v * v, -1, keepdims=True) + 1e-06)
        return v * inv, inv

    def normalise(raw, put):
        def body(i):
            rows = pl.ds(pl.multiple_of(i * 32, 32), 32)
            put(i, rows, unit_rows(raw, rows)[0].astype(BF16))

        loop(ROWS // 32, body)

    def put_ring(i, rows, u):
        ring_r[z, rows, :] = u

    def put_cross(i, rows, u):
        cross_m[pl.ds(pl.multiple_of(q * ROWS + i * 32, 32), 32), :] = u

    loads[0].wait()
    normalise(route_ref, put_ring)
    tcross[q] = jnp.concatenate(
        [target_ref[...].astype(F32), jnp.zeros((1, 256 - ROWS), F32)], axis=1
    )

    pl.semaphore_wait(barrier, len(partners))

    def exists(d, k, h):
        return k < 3 or (k == 3 and h // 2 == d)

    def ring_copy(d, k, h, slot):
        i = (d * 4 + k) * 4 + h
        part = ring_r.at[slot, pl.ds(*PIECES[h])]
        dev = zpeer[0] if d == 0 else zpeer[6]
        return remote(part, part, ring_ss.at[i], ring_rs.at[i], dev)

    def ring_send(d, k, h):
        cp = ring_copy(d, k, h, wrap(z - k, 8) if d == 0 else wrap(z + k, 8))
        cp.start()
        sent.append(cp)

    def ring_wait(d, k, h):
        ring_copy(d, k, h, wrap(z - 1 - k, 8) if d == 0 else wrap(z + 1 + k, 8)).wait_recv()

    order_of = ((0, 1, 2, 3), (2, 3, 0, 1))

    def advance(k, places=(0, 1, 2, 3)):
        for o in places:
            for d in (0, 1):
                h = order_of[d][o]
                if exists(d, k, h):
                    ring_wait(d, k, h)
                    if exists(d, k + 1, h):
                        ring_send(d, k + 1, h)

    def ring_open():
        for o in range(4):
            for d in (0, 1):
                ring_send(d, 0, order_of[d][o])

    b_own, b_sib = block(q), block(2 * y + 1 - c)
    b_across, b_diag = block(2 * (1 - y) + c), block(2 * (1 - y) + 1 - c)

    def cross_copy(i, blk, dev):
        part = cross_m.at[blk]
        return remote(part, part, cross_ss.at[i], cross_rs.at[i], dev)

    def cross_send(i):
        cp = cross_copy(i, b_across if i == 2 else b_own, across if i == 0 else sib)
        cp.start()
        sent.append(cp)

    def cross_wait(i):
        cross_copy(i, (b_across, b_sib, b_diag)[i], sib).wait_recv()

    ring_open()
    loads[1].wait()
    normalise(mol_ref, put_cross)
    cross_send(0)
    for i, dev in enumerate((across, sib, diag)):
        send(tcross.at[q], tcross.at[q], t_ss.at[i], t_rs.at[i], dev)
    cross_send(1)

    loads[2].wait()
    for t in range(16):
        tile = act_ref[:, 128 * t : 128 * t + 128].astype(F32)
        act_t[128 * t : 128 * t + 128, :] = tile.T

    def order(j):
        vv, xx = lax.div(j, 4), lax.rem(j, 4)
        yy, nn = lax.div(vv, 2), lax.rem(vv, 2) * 4 + xx
        for h in (0, 1):
            rows = [
                act_t[pl.ds(pl.multiple_of(1024 * yy + 128 * zz + 64 * h + 8 * nn, 8), 8), :]
                for zz in range(8)
            ]
            act_own[h, vv, xx] = jnp.concatenate(rows, axis=0).astype(BF16)

    loop(16, order)

    acts = (act_x, act_y)
    molds = (mold_x, mold_y)

    def act_part(l, h, at):
        return act_own.at[h, :, at] if l == 0 else act_own.at[h, at]

    own_acts = [
        pltpu.make_async_copy(act_part(l, c, line_at[l]), acts[l].at[line_at[l], c], in_s.at[3 + l])
        for l in (0, 1)
    ]
    for cp in own_acts:
        cp.start()

    def act_send(l):
        here = acts[l].at[line_at[l], c]
        for k in range(4):
            for o in (0, 1):
                if k + o > 0:
                    i = l * 8 + k * 2 + o
                    cc = c if o == 0 else 1 - c
                    src = act_part(l, cc, wrap(line_at[l] + k, 4))
                    send(src, here, act_ss.at[i], act_rs.at[i], line_peer[l](k, cc))

    def act_wait():
        for cp in own_acts:
            cp.wait()
        for l in (0, 1):
            for k in range(4):
                for o in (0, 1):
                    if k + o > 0:
                        i = l * 8 + k * 2 + o
                        cc = c if o == 0 else 1 - c
                        dst = acts[l].at[wrap(line_at[l] - k, 4), cc]
                        remote(dst, dst, act_ss.at[i], act_rs.at[i], sib).wait_recv()

    def mold_copy(l, k, o, j, p, cc, dev):
        i = ((l * 4 + k) * 2 + o) * 3 + j
        at = molds[l].at[p, cc, pl.ds(*CHUNKS[j])]
        return remote(at, at, mold_ss.at[i], mold_rs.at[i], dev)

    def mold_send(l, k, o, j):
        if o == 0:
            cp = mold_copy(l, k, o, j, line_at[l], c, line_peer[l](k, c))
        else:
            cp = mold_copy(l, k, o, j, wrap(line_at[l] - k, 4), c, sib)
        cp.start()
        sent.append(cp)

    def mold_wait(l, k, o, j):
        cc = c if o == 0 else 1 - c
        mold_copy(l, k, o, j, wrap(line_at[l] - k, 4), cc, sib).wait_recv()

    def mold_round(j):
        for k in (2, 1, 3):
            for l in (0, 1):
                mold_send(l, k, 0, j)
        for l in (0, 1):
            mold_send(l, 0, 1, j)

    def mold_pass(j):
        for k in (1, 3, 2):
            for l in (0, 1):
                mold_wait(l, k, 0, j)
                mold_send(l, k, 1, j)

    advance(0)
    cross_wait(0)
    cross_send(2)

    for i, slot in enumerate((2 * (1 - y) + c, 2 * y + 1 - c, 2 * (1 - y) + 1 - c)):
        remote(
            tcross.at[slot], tcross.at[slot], t_ss.at[i], t_rs.at[i], sib
        ).wait_recv()
    eye = lax.broadcasted_iota(jnp.int32, (ROWS, ROWS), 0) == lax.broadcasted_iota(
        jnp.int32, (ROWS, ROWS), 1
    )
    for i in range(4):
        line = jnp.broadcast_to(tcross[i, 0:1, 0:ROWS], (ROWS, ROWS))
        col = jnp.sum(jnp.where(eye, line, 0.0), -1, keepdims=True)
        tcol[i * ROWS : (i + 1) * ROWS, :] = jnp.broadcast_to(col, (ROWS, 128))

    cross_wait(1)
    cross_wait(2)

    shift = shift_ref[0]
    seed = seed_ref[0]

    def pairs(k, first=False):
        slot = wrap(z + k, 8)
        right = ring_r[slot]
        sharp = jnp.exp(jnp.full((1, ROWS), sharp_ref[0], F32))
        ids = lax.broadcasted_iota(jnp.int32, (1, ROWS), 1) + wide_of(y, slot, c) * ROWS
        ids = ids.astype(F32)
        blocks = [pl.ds(i * ROWS, ROWS) for i in range(4)]

        def grads(b, s):
            match = tcol[b, 0:1] == ids
            g = jax.nn.sigmoid(s * sharp + shift) - jnp.where(match, 1.0, 0.0)
            return (seed * g).astype(BF16)

        scores = [
            lax.dot_general(cross_m[b, :], right, NT, preferred_element_type=F32) for b in blocks
        ]
        gs = [grads(b, s) for b, s in zip(blocks, scores)]
        for b, g in zip(blocks, gs):
            out = lax.dot_general(g, right, NN, preferred_element_type=F32)
            if first:
                part_m[b, :] = out
            else:
                part_m[b, :] += out
        part_r[slot] = lax.dot_general(
            jnp.concatenate(gs, axis=0), cross_m[...], TN, preferred_element_type=F32
        )

    def back_copy(d, s, h):
        rows = pl.ds(h * HALF, HALF)
        i = (d * 4 + s) * 2 + h
        dev = zpeer[0] if d == 0 else zpeer[6]
        return remote(
            back_out.at[d, s, rows], back_in.at[d, s, rows], back_ss.at[i], back_rs.at[i], dev
        )

    def back_send(d, s, h):
        far = h == d
        k = 4 - s if d == 0 else 4 + s
        goal = wrap(z + k, 8)
        carried = s >= (1 if far else 2)
        if carried:
            back_copy(d, s - 1, h).wait_recv()
        spread = jnp.zeros((1, 256), F32)
        for first in range(h * HALF, h * HALF + HALF, 16):
            rows = pl.ds(first, 16)
            total = part_r[goal, rows, :]
            if carried:
                total += back_in[d, s - 1, rows, :].astype(F32)
            unit = ring_r[goal, rows, :].astype(F32)
            along = jnp.sum(total * unit, -1, keepdims=True)
            back_out[d, s, rows, :] = (total - along * unit).astype(BF16)
            place = lax.broadcasted_iota(jnp.int32, (16, 256), 0) + first
            place = place == lax.broadcasted_iota(jnp.int32, (16, 256), 1)
            spread += jnp.sum(jnp.where(place, along, 0.0), 0, keepdims=True)
        cp = back_copy(d, s, h)
        cp.start()
        sent.append(cp)
        if (d == 0) if s == 0 else not far:
            back_along[goal] = spread
        else:
            back_along[goal] += spread
            send(
                back_along.at[goal],
                along_in.at[z],
                along_ss.at[k - 1],
                along_rs.at[k - 1],
                zpeer[k - 1],
            )

    def back_near(s):
        back_send(0, s, 1)
        back_send(1, s, 0)

    def back_far(s):
        back_send(0, s, 0)
        back_send(1, s, 1)

    def back_close():
        for h in (1, 0):
            back_copy(0, 3, h).wait_recv()
            back_copy(1, 3, 1 - h).wait_recv()
        line = jnp.zeros((1, 256), F32)
        for k in range(1, 8):
            at = along_in.at[wrap(z - k, 8)]
            remote(at, at, along_ss.at[k - 1], along_rs.at[k - 1], sib).wait_recv()
            line += along_in[wrap(z - k, 8)]

        def body(i):
            rows = pl.ds(pl.multiple_of(i * 32, 32), 32)
            total = part_r[z, rows, :]
            for d in (0, 1):
                total += back_in[d, 3, rows, :].astype(F32)
            along = jnp.sum(jnp.where(diagonal(i), line[:, :ROWS], 0.0), -1, keepdims=True)
            total += along * ring_r[z, rows, :].astype(F32)
            route_out[rows, :] = norm_back(route_ref, rows, total)

        loop(ROWS // 32, body)

    def reduce_copy(i, j):
        rows = pl.ds(*CHUNKS[j])
        dev = sib
        if i < 2:
            q_ = 2 * (1 - y) + 1 - c if i == 0 else 2 * y + 1 - c
            here = pl.ds(pl.multiple_of(q_ * ROWS + CHUNKS[j][0], 32), CHUNKS[j][1])
            src, dst = part_m.at[here], sib_in.at[i, rows]
        elif i == 2:
            src, dst, dev = y_out.at[rows], y_in.at[rows], across
        else:
            src, dst, dev = a_out.at[j], a_in.at[j], across
        i = i * 3 + j
        return remote(src, dst, red_ss.at[i], red_rs.at[i], dev)

    def reduce_send(i, j):
        cp = reduce_copy(i, j)
        cp.start()
        sent.append(cp)

    def reduce_open():
        for i in (0, 1):
            for j in (0, 1, 2):
                reduce_send(i, j)

    def diagonal(i):
        row = lax.broadcasted_iota(jnp.int32, (32, ROWS), 0) + i * 32
        return row == lax.broadcasted_iota(jnp.int32, (32, ROWS), 1)

    def norm_back(raw, rows, total):
        unit, inv = unit_rows(raw, rows)
        sharp = jnp.exp(jnp.full((32, 1), sharp_ref[0], F32))
        along = jnp.sum(unit * total, -1, keepdims=True)
        return ((total - unit * along) * (inv * sharp)).astype(BF16)

    def blocks_of(j, body):
        first, size = CHUNKS[j]
        loop(size // 32, lambda i: body(i + first // 32))

    def reduce_across(j):
        a_out[j] = jnp.zeros((8, ROWS), F32)
        reduce_copy(0, j).wait_recv()

        def body(i):
            rows = pl.ds(pl.multiple_of(i * 32, 32), 32)
            far = pl.ds(pl.multiple_of((2 * (1 - y) + c) * ROWS + i * 32, 32), 32)
            total = part_m[far, :] + sib_in[0, rows, :]
            unit = cross_m[far, :].astype(F32)
            along = jnp.sum(total * unit, -1, keepdims=True)
            y_out[rows, :] = (total - along * unit).astype(BF16)
            spread = jnp.sum(jnp.where(diagonal(i), along, 0.0), 0, keepdims=True)
            a_out[j] += jnp.broadcast_to(spread, (8, ROWS))

        blocks_of(j, body)
        reduce_send(2, j)
        reduce_send(3, j)

    def reduce_close(j):
        for i in (1, 2, 3):
            reduce_copy(i, j).wait_recv()

        def body(i):
            rows = pl.ds(pl.multiple_of(i * 32, 32), 32)
            own = pl.ds(pl.multiple_of(q * ROWS + i * 32, 32), 32)
            total = part_m[own, :] + sib_in[1, rows, :] + y_in[rows, :].astype(F32)
            along = jnp.sum(jnp.where(diagonal(i), a_in[j, 0:1, :], 0.0), -1, keepdims=True)
            total = total + along * cross_m[own, :].astype(F32)
            value = norm_back(mol_ref, rows, total)
            mold_x[x, c, rows, :] = value[:, : D // 2]
            mold_y[v, c, rows, :] = value[:, D // 2 :]

        blocks_of(j, body)
        mold_round(j)

    act_send(0)
    act_send(1)
    pairs(0, True)
    pairs(-1)
    advance(1, (0, 1))
    pairs(1)
    advance(1, (2, 3))
    pairs(-2)
    advance(2, (0, 1))
    pairs(2)
    advance(2, (2, 3))
    pairs(-3)
    pairs(3)
    back_near(1)
    advance(3)
    pairs(4)

    reduce_open()
    back_far(0)
    reduce_across(0)
    reduce_across(1)
    reduce_across(2)
    back_near(2)
    reduce_close(0)
    back_far(1)
    reduce_close(1)
    reduce_close(2)
    back_near(3)
    mold_pass(0)
    back_far(2)
    mold_pass(1)
    mold_pass(2)
    act_wait()
    back_far(3)
    for j in (0, 1, 2):
        for k in (0, 1, 3, 2):
            for l in (0, 1):
                mold_wait(l, k, 1, j)

    def weight(l, half):
        total = jnp.zeros((256, 256), F32)
        for p in range(4):
            for cc in (0, 1):
                total += lax.dot_general(
                    acts[l][p, cc].reshape(256, ROWS),
                    molds[l][p, cc, :, 256 * half : 256 * half + 256],
                    NN,
                    preferred_element_type=F32,
                )
        total = total.reshape(4, 64, 256)
        prod[l, half] = total
        wsend[l, half] = total.astype(BF16)

    def weight_copy(l, half, k, src, slot):
        i = (l * 2 + half) * 3 + k - 1
        dst = wrecv.at[l, half, slot]
        return remote(src, dst, w_ss.at[i], w_rs.at[i], line_peer[1 - l](k, c))

    for half in (0, 1):
        for l in (0, 1):
            weight(l, half)
            here = line_at[1 - l]
            for k in (2, 1, 3):
                src = wsend.at[l, half, wrap(here + k, 4)]
                cp = weight_copy(l, half, k, src, here)
                cp.start()
                sent.append(cp)

    for half in (0, 1):
        for l in (0, 1):
            for k in (1, 3, 2):
                slot = wrap(line_at[1 - l] - k, 4)
                weight_copy(l, half, k, wrecv.at[l, half, slot], slot).wait_recv()

    def gather_sum(i):
        rows = pl.ds(pl.multiple_of(i * 16, 16), 16)
        for half in (0, 1):
            cols = slice(256 * half, 256 * half + 256)
            lines = []
            for l in (0, 1):
                total = prod[l, half, line_at[1 - l], rows, :]
                for k in (1, 2, 3):
                    total += wrecv[l, half, wrap(line_at[1 - l] - k, 4), rows, :].astype(F32)
                lines.append(total)
            for o in (0, 1):
                both = jnp.concatenate([total[8 * o : 8 * o + 8, :] for total in lines], axis=0)
                zown[2 * i + o, :, cols] = both
                zsend[2 * i + o, :, cols] = both.astype(BF16)

    loop(4, gather_sum)
    for k in range(1, 8):
        src = zsend.at[wrap(z + k, 8)]
        send(src, zrecv.at[z], z_ss.at[k - 1], z_rs.at[k - 1], zpeer[k - 1])
    back_close()
    total = zown[z]
    for k in range(1, 8):
        at = zrecv.at[wrap(z - k, 8)]
        remote(at, at, z_ss.at[k - 1], z_rs.at[k - 1], sib).wait_recv()
        total += zrecv[wrap(z - k, 8)].astype(F32)
    gath[n] = total.astype(BF16)
    for k in (4, 2, 6, 1, 3, 5, 7):
        dev = (w, lax.rem(n + k, 8))
        send(gath.at[n], gath.at[n], g_ss.at[k - 1], g_rs.at[k - 1], dev)

    for k in range(1, 8):
        at = gath.at[lax.rem(n - k + 8, 8)]
        remote(at, at, g_ss.at[k - 1], g_rs.at[k - 1], sib).wait_recv()
    for i in range(8):
        total = gath[i].astype(F32)
        weight_out[8 * i : 8 * i + 8, : D // 2] = total[0:8, :]
        weight_out[8 * i : 8 * i + 8, D // 2 :] = total[8:16, :]
    for cp in sent:
        cp.wait_send()


def local(
    compound_activation,
    compound_vectors,
    pathway_vectors,
    matching_pathway_index,
    exponent_of_sharpness,
    offset_shift,
    objective_seed,
):
    vmem = pl.BlockSpec(memory_space=pltpu.VMEM)
    hbm = pl.BlockSpec(memory_space=pltpu.HBM)
    smem = pl.BlockSpec(memory_space=pltpu.SMEM)
    dma = pltpu.SemaphoreType.DMA
    weight_grad, route_grad = pl.pallas_call(
        kernel,
        out_shape=(
            pltpu.VMEM((64, D), F32),
            pltpu.VMEM((ROWS, D), BF16),
        ),
        in_specs=[hbm] * 3 + [vmem] + [smem] * 3,
        out_specs=(vmem, vmem),
        scratch_shapes=[
            pltpu.VMEM((ROWS, FF), BF16),
            pltpu.VMEM((ROWS, D), BF16),
            pltpu.VMEM((ROWS, D), BF16),
            pltpu.VMEM((8, ROWS, D), BF16),
            pltpu.VMEM((4 * ROWS, D), BF16),
            pltpu.VMEM((4, 1, 256), F32),
            pltpu.VMEM((4 * ROWS, 128), F32),
            pltpu.VMEM((4 * ROWS, D), F32),
            pltpu.VMEM((8, ROWS, D), F32),
            pltpu.VMEM((2, 4, ROWS, D), BF16),
            pltpu.VMEM((2, 4, ROWS, D), BF16),
            pltpu.VMEM((8, 1, 256), F32),
            pltpu.VMEM((8, 1, 256), F32),
            pltpu.VMEM((2, ROWS, D), F32),
            pltpu.VMEM((ROWS, D), BF16),
            pltpu.VMEM((ROWS, D), BF16),
            pltpu.VMEM((3, 8, ROWS), F32),
            pltpu.VMEM((3, 8, ROWS), F32),
            pltpu.VMEM((FF, ROWS), F32),
            pltpu.VMEM((2, 4, 4, 64, ROWS), BF16),
            pltpu.VMEM((4, 2, 4, 64, ROWS), BF16),
            pltpu.VMEM((4, 2, 4, 64, ROWS), BF16),
            pltpu.VMEM((4, 2, ROWS, D // 2), BF16),
            pltpu.VMEM((4, 2, ROWS, D // 2), BF16),
            pltpu.VMEM((2, 2, 4, 64, D // 4), F32),
            pltpu.VMEM((2, 2, 4, 64, D // 4), BF16),
            pltpu.VMEM((2, 2, 4, 64, D // 4), BF16),
            pltpu.VMEM((8, 16, D // 2), F32),
            pltpu.VMEM((8, 16, D // 2), BF16),
            pltpu.VMEM((8, 16, D // 2), BF16),
            pltpu.VMEM((8, 16, D // 2), BF16),
            dma((32,)),
            dma((32,)),
            dma((16,)),
            dma((16,)),
            dma((7,)),
            dma((7,)),
            dma((3,)),
            dma((3,)),
            dma((3,)),
            dma((3,)),
            dma((12,)),
            dma((12,)),
            dma((5,)),
            dma((16,)),
            dma((16,)),
            dma((48,)),
            dma((48,)),
            dma((12,)),
            dma((12,)),
            dma((7,)),
            dma((7,)),
            dma((7,)),
            dma((7,)),
        ],
        compiler_params=pltpu.CompilerParams(
            collective_id=0, has_side_effects=True, vmem_limit_bytes=60 * 1024 * 1024
        ),
        name="contrastive_backward",
    )(
        compound_activation[0],
        compound_vectors[0],
        pathway_vectors[0],
        matching_pathway_index,
        exponent_of_sharpness,
        offset_shift,
        objective_seed,
    )
    return weight_grad, route_grad[None]


def solution(mesh):
    in_specs = (
        P("narrow", "wide", None),
        P("narrow", "wide", None),
        P("narrow", "wide", None),
        P("narrow", "wide"),
        P(),
        P(),
        P(),
    )
    out_specs = (P("wide", None), P("narrow", "wide", None))
    return jax.shard_map(local, mesh=mesh, in_specs=in_specs, out_specs=out_specs, check_vma=False)
```

time: 85 us -> 84.4 us (level); the launches traced: 83.6 us -> 84.3 us
  no operation moved by 1% of the time
where the time goes in v4:
time: 84.4 us; the launch traced here: 84.3 us
  Pallas kernels  80.3 us (95%)
  between operations  2.58 us (3%)
  local copies, waits for them, and re-layouts  1.43 us (2%)
    pallas_call x1, Pallas kernels, local(): pl.pallas_call(kernel, out_shape=(pltpu.VMEM((64, D), F32), pltpu.VMEM((R...  80.3 us

profile of v4, /device:TPU:2, one launch (start us, length us, event | category | flops | bytes accessed | tf_op | source)
XLA Modules:
  0.0 84.3 jit_solution(12640172484704932597)
XLA Ops:
  2.6 80.3 %contrastive_backward.1 = (f32[64,1024]{1,0:T(8,128)S(1)}, bf16[160,1024]{1,0:T(8,128)(2,1)S(1)}) custom-call(bf16[160,2048]{1,0:T(8,128)(2,1)} %bitcast.5, bf16[160,1024]{1,0:T(8,128)(2,1)} %bitcast.6, bf16[160,1024]{1,0:T(8,128)(2,1)} %bitcast.7, s32[1,160]{1,0:T(1,128)} %target_ref.1, f32[1]{0:T(128)S(6)} %copy.13.sharp_ref, f32[1]{0:T(128)S(6)} %copy.14.shift_ref, ...), custom_call_target="tpu_custom_call" | custom-call | tf_op jit(solution)/shard_map/contrastive_backward/pallas_call | solution.py:642
  82.9 0.7 copy.11
  83.6 0.7 copy.12

commit v5 on v4

--- a/solution.py
+++ b/solution.py
@@ -544,7 +544,6 @@
     mold_pass(1)
     mold_pass(2)
     act_wait()
-    back_far(3)
     for j in (0, 1, 2):
         for k in (0, 1, 3, 2):
             for l in (0, 1):
@@ -578,6 +577,8 @@
                 cp = weight_copy(l, half, k, src, here)
                 cp.start()
                 sent.append(cp)
+
+    back_far(3)
 
     for half in (0, 1):
         for l in (0, 1):
@@ -601,20 +602,20 @@
                 zsend[2 * i + o, :, cols] = both.astype(BF16)
 
     loop(4, gather_sum)
-    for k in range(1, 8):
+    for k in (4, 3, 5, 2, 6, 1, 7):
         src = zsend.at[wrap(z + k, 8)]
         send(src, zrecv.at[z], z_ss.at[k - 1], z_rs.at[k - 1], zpeer[k - 1])
-    back_close()
     total = zown[z]
     for k in range(1, 8):
         at = zrecv.at[wrap(z - k, 8)]
         remote(at, at, z_ss.at[k - 1], z_rs.at[k - 1], sib).wait_recv()
         total += zrecv[wrap(z - k, 8)].astype(F32)
     gath[n] = total.astype(BF16)
-    for k in (4, 2, 6, 1, 3, 5, 7):
+    for k in (6, 2, 5, 7, 1, 3, 4):
         dev = (w, lax.rem(n + k, 8))
         send(gath.at[n], gath.at[n], g_ss.at[k - 1], g_rs.at[k - 1], dev)
 
+    back_close()
     for k in range(1, 8):
         at = gath.at[lax.rem(n - k + 8, 8)]
         remote(at, at, g_ss.at[k - 1], g_rs.at[k - 1], sib).wait_recv()

time: 84.4 us -> 82.8 us (0.981)
  Pallas kernels: 80.3 us -> 78 us
    pallas_call x1, Pallas kernels: 80.3 us -> 78 us  [local(): pl.pallas_call(kernel, out_shape=(pltpu.VMEM((64, D), F32), pltpu.VMEM((R...]
where the time goes in v5:
time: 82.8 us; the launch traced here: 82 us
  Pallas kernels  78 us (94%)
  between operations  2.58 us (3%)
  local copies, waits for them, and re-layouts  1.43 us (2%)
    pallas_call x1, Pallas kernels, local(): pl.pallas_call(kernel, out_shape=(pltpu.VMEM((64, D), F32), pltpu.VMEM((R...  78 us

profile of v5, /device:TPU:2, one launch (start us, length us, event | category | flops | bytes accessed | tf_op | source)
XLA Modules:
  0.0 82.0 jit_solution(13618967079141482070)
XLA Ops:
  2.6 78.0 %contrastive_backward.1 = (f32[64,1024]{1,0:T(8,128)S(1)}, bf16[160,1024]{1,0:T(8,128)(2,1)S(1)}) custom-call(bf16[160,2048]{1,0:T(8,128)(2,1)} %bitcast.5, bf16[160,1024]{1,0:T(8,128)(2,1)} %bitcast.6, bf16[160,1024]{1,0:T(8,128)(2,1)} %bitcast.7, s32[1,160]{1,0:T(1,128)} %target_ref.1, f32[1]{0:T(128)S(6)} %copy.13.sharp_ref, f32[1]{0:T(128)S(6)} %copy.14.shift_ref, ...), custom_call_target="tpu_custom_call" | custom-call | tf_op jit(solution)/shard_map/contrastive_backward/pallas_call | solution.py:643
  80.6 0.7 copy.11
  81.3 0.7 copy.12

commit v6 on v5

--- a/solution.py
+++ b/solution.py
@@ -7,7 +7,7 @@
 
 ROWS = 160
 PIECES = ((0, 48), (48, 32), (80, 48), (128, 32))
-CHUNKS = ((0, 64), (64, 64), (128, 32))
+CHUNKS = ((0, 32), (32, 64), (96, 32), (128, 32))
 D = 1024
 FF = 2048
 HALF = 80
@@ -289,7 +289,7 @@
                         remote(dst, dst, act_ss.at[i], act_rs.at[i], sib).wait_recv()
 
     def mold_copy(l, k, o, j, p, cc, dev):
-        i = ((l * 4 + k) * 2 + o) * 3 + j
+        i = ((l * 4 + k) * 2 + o) * 4 + j
         at = molds[l].at[p, cc, pl.ds(*CHUNKS[j])]
         return remote(at, at, mold_ss.at[i], mold_rs.at[i], dev)
 
@@ -340,7 +340,7 @@
     shift = shift_ref[0]
     seed = seed_ref[0]
 
-    def pairs(k, first=False):
+    def pairs(k, first=False, between=None):
         slot = wrap(z + k, 8)
         right = ring_r[slot]
         sharp = jnp.exp(jnp.full((1, ROWS), sharp_ref[0], F32))
@@ -363,6 +363,8 @@
                 part_m[b, :] = out
             else:
                 part_m[b, :] += out
+        if between is not None:
+            between()
         part_r[slot] = lax.dot_general(
             jnp.concatenate(gs, axis=0), cross_m[...], TN, preferred_element_type=F32
         )
@@ -449,7 +451,7 @@
             src, dst, dev = y_out.at[rows], y_in.at[rows], across
         else:
             src, dst, dev = a_out.at[j], a_in.at[j], across
-        i = i * 3 + j
+        i = i * 4 + j
         return remote(src, dst, red_ss.at[i], red_rs.at[i], dev)
 
     def reduce_send(i, j):
@@ -459,7 +461,7 @@
 
     def reduce_open():
         for i in (0, 1):
-            for j in (0, 1, 2):
+            for j in (0, 1, 2, 3):
                 reduce_send(i, j)
 
     def diagonal(i):
@@ -526,25 +528,27 @@
     pairs(3)
     back_near(1)
     advance(3)
-    pairs(4)
-
-    reduce_open()
+    pairs(4, between=reduce_open)
+
     back_far(0)
     reduce_across(0)
     reduce_across(1)
     reduce_across(2)
+    reduce_across(3)
     back_near(2)
     reduce_close(0)
     back_far(1)
     reduce_close(1)
     reduce_close(2)
+    reduce_close(3)
     back_near(3)
     mold_pass(0)
     back_far(2)
     mold_pass(1)
     mold_pass(2)
+    mold_pass(3)
     act_wait()
-    for j in (0, 1, 2):
+    for j in (0, 1, 2, 3):
         for k in (0, 1, 3, 2):
             for l in (0, 1):
                 mold_wait(l, k, 1, j)
@@ -665,8 +669,8 @@
             pltpu.VMEM((2, ROWS, D), F32),
             pltpu.VMEM((ROWS, D), BF16),
             pltpu.VMEM((ROWS, D), BF16),
-            pltpu.VMEM((3, 8, ROWS), F32),
-            pltpu.VMEM((3, 8, ROWS), F32),
+            pltpu.VMEM((4, 8, ROWS), F32),
+            pltpu.VMEM((4, 8, ROWS), F32),
             pltpu.VMEM((FF, ROWS), F32),
             pltpu.VMEM((2, 4, 4, 64, ROWS), BF16),
             pltpu.VMEM((4, 2, 4, 64, ROWS), BF16),
@@ -690,13 +694,13 @@
             dma((3,)),
             dma((3,)),
             dma((3,)),
-            dma((12,)),
-            dma((12,)),
+            dma((16,)),
+            dma((16,)),
             dma((5,)),
             dma((16,)),
             dma((16,)),
-            dma((48,)),
-            dma((48,)),
+            dma((64,)),
+            dma((64,)),
             dma((12,)),
             dma((12,)),
             dma((7,)),

time: 82.8 us -> 82.7 us (level)
  no operation moved by 1% of the time
where the time goes in v6:
time: 82.7 us; the launch traced here: 81.9 us
  Pallas kernels  77.9 us (94%)
  between operations  2.58 us (3%)
  local copies, waits for them, and re-layouts  1.43 us (2%)
    pallas_call x1, Pallas kernels, local(): pl.pallas_call(kernel, out_shape=(pltpu.VMEM((64, D), F32), pltpu.VMEM((R...  77.9 us

profile of v6, /device:TPU:2, one launch (start us, length us, event | category | flops | bytes accessed | tf_op | source)
XLA Modules:
  0.0 81.9 jit_solution(11109554838922504330)
XLA Ops:
  2.6 77.9 %contrastive_backward.1 = (f32[64,1024]{1,0:T(8,128)S(1)}, bf16[160,1024]{1,0:T(8,128)(2,1)S(1)}) custom-call(bf16[160,2048]{1,0:T(8,128)(2,1)} %bitcast.5, bf16[160,1024]{1,0:T(8,128)(2,1)} %bitcast.6, bf16[160,1024]{1,0:T(8,128)(2,1)} %bitcast.7, s32[1,160]{1,0:T(1,128)} %target_ref.1, f32[1]{0:T(128)S(6)} %copy.13.sharp_ref, f32[1]{0:T(128)S(6)} %copy.14.shift_ref, ...), custom_call_target="tpu_custom_call" | custom-call | tf_op jit(solution)/shard_map/contrastive_backward/pallas_call | solution.py:647
  80.5 0.7 copy.11
  81.2 0.7 copy.12
